TPU v7x, 32 devices: a whole 2x2x4 slice. The times are simulated.
32 devices in a mesh: path: 4 (over x, core), ctx: 8 (over z, y).
Axes of the slice: x: 2, y: 2, z: 4, core: 2. Of those that a mesh axis runs over, the one named last changes fastest.
Arguments:
- tokens: int32 [1024], P('ctx'), may hold values from 0 to 511
- sub_pos: int32 [128], P('ctx'), may hold values from 0 to 1023, as said below
- sub_base: int32 [128], P('ctx'), may hold values from 0 to 511
- embed: bfloat16 [512, 4096], replicated, may hold values from -6 to 6
- norm_gain: float32 [4096], replicated, may hold values from 0.1 to 1.9
- fir_taps: bfloat16 [3, 3, 4096], replicated, may hold values from -3.5 to 3.5
- long_filter: float32 [1024, 4096], P(None, 'ctx'), may hold values from -8 to 8
- skip_gain: float32 [4096], P('ctx'), may hold values from 0.5 to 1.5
- cotangent: bfloat16 [1024, 4096], P('ctx'), may hold values from -6 to 6
Outputs:
- path_grad: float32 [1024, 4096], P('ctx', 'path')
- attribution: float32 [1024, 4096], P('ctx', 'path')
Inputs may be any that keep to these rules, and one draw needn't show every extreme that they name: `sub_pos`: exactly one substituted position in each aligned block of 8 tokens, so the positions rise strictly.
All inputs are finite; a program needn't handle non-finite values.
Results may differ from a plain program's by a relative error of at most 0.0085.
Values may be sent and summed in bfloat16 or wider, within the bound.
No kernel may reach another device: no remote copies, remote signals or barrier semaphores. Data moves between devices by JAX's collectives and lax.ppermute only.
A program may use at most 192 MiB of HBM per device.

v0:
```python
import functools

import jax
import jax.numpy as jnp
import ml_dtypes
import numpy as np
from jax import lax
from jax.experimental import pallas as pl
from jax.experimental.pallas import tpu as pltpu
from jax.sharding import PartitionSpec as P

LANES = 128
GROUP = 8
RADIX = 4
LOOK_ROWS = 256
CHUNK = 16
EPS = 1e-06
CANCEL = 0.004
TABLE_BYTES = 2**21
F32 = jnp.float32
BF16 = jnp.bfloat16
precise = lax.Precision.HIGH


def angle_tables(length):
    outer_size = 64
    inner_size = length // outer_size
    outer_idx = jnp.arange(outer_size, dtype=jnp.int32)
    inner_idx = jnp.arange(inner_size, dtype=jnp.int32)
    outer_angle = (
        2.0 * jnp.pi / outer_size
        * (outer_idx[:, None] * outer_idx[None, :] % outer_size).astype(F32)
    )
    inner_angle = (
        2.0 * jnp.pi / inner_size
        * (inner_idx[:, None] * inner_idx[None, :] % inner_size).astype(F32)
    )
    twist_angle = (
        2.0 * jnp.pi / length
        * (outer_idx[:, None] * inner_idx[None, :] % length).astype(F32)
    )
    return (outer_angle, inner_angle, twist_angle)


def complex_table(angle, sign):
    cosine = jnp.cos(angle)
    sine = sign * jnp.sin(angle)
    return jnp.stack([jnp.stack([cosine, sine]), jnp.stack([-sine, cosine])])


def twisted(values, angle, sign):
    cosine = jnp.cos(angle)[None, :, :, None]
    sine = sign * jnp.sin(angle)[None, :, :, None]
    real_part = values[:, 0]
    imag_part = values[:, 1]
    return jnp.stack(
        [real_part * cosine - imag_part * sine, real_part * sine + imag_part * cosine], 1
    )


def spectrum(signal):
    batch, half, width = signal.shape
    length = 2 * half
    outer_angle, inner_angle, twist_angle = angle_tables(length)
    outer_size = outer_angle.shape[0]
    inner_size = inner_angle.shape[0]
    folded = signal.reshape(batch, outer_size // 2, inner_size, width)
    used = outer_angle[:, : outer_size // 2]
    outer_table = jnp.stack([jnp.cos(used), -jnp.sin(used)])
    first = jnp.einsum("rka,pabc->prkbc", outer_table, folded, precision=precise)
    turned = twisted(first, twist_angle, -1.0)
    return jnp.einsum(
        "prkbc,rsbm->pskmc", turned, complex_table(inner_angle, -1.0), precision=precise
    )


def inverse(spec):
    batch, parts, outer_size, inner_size, width = spec.shape
    length = outer_size * inner_size
    outer_angle, inner_angle, twist_angle = angle_tables(length)
    back = jnp.einsum("pskmc,stmb->ptkbc", spec, complex_table(inner_angle, 1.0), precision=precise)
    turned = twisted(back, twist_angle, 1.0)
    used = outer_angle[: outer_size // 2]
    outer_table = jnp.stack([jnp.cos(used), -jnp.sin(used)])
    result = jnp.einsum("rak,prkbc->pabc", outer_table, turned, precision=precise)
    return (result / length).reshape(batch, length // 2, width)


def long_conv(signal, filter_spec, skip_gain, adjoint):
    spec = spectrum(signal)
    sig_real = spec[:, 0]
    sig_imag = spec[:, 1]
    filt_real = filter_spec[:, 0]
    filt_imag = filter_spec[:, 1]
    if adjoint:
        prod_real = sig_real * filt_real + sig_imag * filt_imag
        prod_imag = sig_imag * filt_real - sig_real * filt_imag
    else:
        prod_real = sig_real * filt_real - sig_imag * filt_imag
        prod_imag = sig_real * filt_imag + sig_imag * filt_real
    return inverse(jnp.stack([prod_real, prod_imag], 1)) + skip_gain * signal


def rounded(value):
    return value.astype(BF16).astype(F32)


def shifted(values, step):
    zeros = jnp.zeros_like(values[:, : abs(step)])
    if step > 0:
        return jnp.concatenate([zeros, values[:, :-step]], 1)
    return jnp.concatenate([values[:, -step:], zeros], 1)


@functools.lru_cache(maxsize=None)
def dft_tables(length):
    quarter = length // RADIX
    freq = 4 * np.arange(quarter, dtype=np.int64) + 1
    place = np.arange(quarter, dtype=np.int64)
    there, back = [], []
    for offset in range(RADIX):
        turns = freq[:, None] * (RADIX * place + offset)[None, :] % (4 * length)
        angle = turns * (2.0 * np.pi / (4 * length))
        cosine = np.cos(angle).astype(ml_dtypes.bfloat16)
        sine = np.sin(angle).astype(ml_dtypes.bfloat16)
        there.append(np.concatenate([cosine, sine], 0))
        back.append(np.concatenate([cosine.T, sine.T], 1))
    return (np.stack(there), np.stack(back))


def butterfly(values, sign):
    (r0, s0), (r1, s1), (r2, s2), (r3, s3) = values
    sum_r, sum_s, diff_r, diff_s = r0 + r2, s0 + s2, r0 - r2, s0 - s2
    odd_r, odd_s, turn_r, turn_s = r1 + r3, s1 + s3, r1 - r3, s1 - s3
    ahead = (diff_r + turn_s, diff_s - turn_r)
    behind = (diff_r - turn_s, diff_s + turn_r)
    if sign < 0:
        ahead, behind = behind, ahead
    return ((sum_r + odd_r, sum_s + odd_s), ahead, (sum_r - odd_r, sum_s - odd_s), behind)


def transposed(rows):
    count = rows.shape[0]
    if count < LANES:
        rows = jnp.concatenate([rows, jnp.zeros((LANES - count, LANES), F32)], 0)
    return rows.T


def dot(left, right):
    return jnp.dot(left, right, preferred_element_type=F32)


def iota(dims, axis):
    return lax.broadcasted_iota(jnp.int32, dims, axis)


def by_residue():
    row = iota((LANES, LANES), 0)
    part = LANES // RADIX
    source = RADIX * (row % part) + row // part
    return (iota((LANES, LANES), 1) == source).astype(F32)


def hot(ids, vocab):
    lane = iota(ids.shape, 1).astype(F32)
    parts = [
        (ids == lane + float(column * LANES)).astype(F32).astype(BF16)
        for column in range(vocab // LANES)
    ]
    return jnp.concatenate(parts, 1)


def joined(block, kind):
    return 256.0 * block[2 * kind : 2 * kind + 1] + block[2 * kind + 1 : 2 * kind + 2]


def pack_kernel(
    tok_hbm, pos_hbm, put_hbm, cot_hbm, msg_ref, ids_ref, tok_ref, pos_ref, put_ref, cot_ref, sems
):
    dests, rows, share = msg_ref.shape
    tok_rows = cot_hbm.shape[0]
    n_path = cot_hbm.shape[1] // (dests * share)
    path = lax.axis_index("path")
    moves = [(tok_hbm, tok_ref), (pos_hbm, pos_ref), (put_hbm, put_ref)]
    for dest in range(dests):
        lanes = pl.ds(pl.multiple_of((dest * n_path + path) * share, LANES), share)
        moves.append((cot_hbm.at[:, lanes], cot_ref.at[:, pl.ds(dest * share, share)]))
    copies = [
        pltpu.make_async_copy(source, target, sems.at[index])
        for index, (source, target) in enumerate(moves)
    ]
    for copy in copies:
        copy.start()
    order = by_residue().astype(BF16)
    for copy in copies[:3]:
        copy.wait()
    lists = []
    for ref in (tok_ref, pos_ref, put_ref):
        value = ref[...].astype(F32)
        if value.shape[1] < LANES:
            value = jnp.concatenate([value, jnp.zeros((1, LANES - value.shape[1]), F32)], 1)
        high = jnp.floor(value * (1.0 / 256.0))
        lists += [high, value - 256.0 * high]
    lists.append(jnp.zeros((rows - tok_rows - len(lists), LANES), F32))
    ids = jnp.concatenate(lists, 0)
    ids_ref[...] = ids
    turned = lax.dot_general(
        ids.astype(BF16), order, (((1,), (1,)), ((), ())), preferred_element_type=F32
    )
    ids = jnp.where(iota(ids.shape, 0) < 2, turned, ids).astype(BF16)
    for dest in range(dests):
        msg_ref[dest, tok_rows:, :] = ids
    for copy in copies[3:]:
        copy.wait()
    turned = dot(order, cot_ref[...]).astype(BF16)
    for dest in range(dests):
        msg_ref[dest, :tok_rows, :] = turned[:, dest * share : (dest + 1) * share]


def prepare_kernel(
    filt_hbm, table_hbm, embed_hbm, skip_hbm, after_ref,
    spec_hbm, gram_hbm,
    filt_ref, table_ref, embed_ref, skip_ref, sum_ref, spec_ref, gram_ref, sems, out_sems,
):
    length, share = filt_ref.shape
    quarter = length // RADIX
    vocab, width = embed_ref.shape
    pieces = sems.shape[0] - 3
    wide = width // pieces
    path = lax.axis_index("path")
    lanes = pl.ds(pl.multiple_of(path * share, LANES), share)
    moves = [
        (filt_hbm.at[:, lanes], filt_ref),
        (skip_hbm.at[:, lanes], skip_ref),
        (table_hbm, table_ref),
    ]
    for index in range(pieces):
        lanes = pl.ds(index * wide, wide)
        moves.append((embed_hbm.at[:, lanes], embed_ref.at[:, lanes]))
    copies = [
        pltpu.make_async_copy(source, target, sems.at[index])
        for index, (source, target) in enumerate(moves)
    ]
    for copy in copies:
        copy.start()

    copies[0].wait()
    copies[1].wait()
    filt_ref[0:1, :] = filt_ref[0:1, :] + skip_ref[...]
    parts = []
    for offset in range(RADIX):
        value = filt_ref[pl.ds(offset, quarter, stride=RADIX), :] * (1.0 / length)
        high = value.astype(BF16)
        parts.append(jnp.concatenate([high, (value - high.astype(F32)).astype(BF16)], 1))
    copies[2].wait()
    found = []
    for offset in range(RADIX):
        both = dot(table_ref[offset], parts[offset])
        both = both[:, :share] + both[:, share:]
        found.append((both[:quarter], both[quarter:]))
    for part, (real, imag) in enumerate(butterfly(found, -1)):
        spec_ref[2 * part] = real
        spec_ref[2 * part + 1] = imag
    outs = [pltpu.make_async_copy(spec_ref, spec_hbm, out_sems.at[0])]
    outs[0].start()

    sum_ref[vocab // 2 :, : vocab // 2] = jnp.zeros((vocab // 2, vocab // 2), F32)
    for index in range(pieces):
        copies[3 + index].wait()
        part = embed_ref[:, index * wide : (index + 1) * wide]
        for rows, lanes in ((slice(0, vocab // 2), slice(0, vocab)), (slice(vocab // 2, vocab),) * 2):
            found = lax.dot_general(
                part[rows], part[lanes], (((1,), (1,)), ((), ())), preferred_element_type=F32
            )
            if index == 0:
                sum_ref[rows, lanes] = found
            else:
                sum_ref[rows, lanes] += found
    first = (lax.axis_index("ctx") * lax.axis_size("path") + path) * share
    mine = embed_ref[:, pl.ds(pl.multiple_of(first, LANES), share)]
    same = iota((LANES, LANES), 0) == iota((LANES, LANES), 1)
    lane = iota((LANES, LANES), 1)
    below = 3 * vocab
    for block in range(vocab // LANES):
        rows = slice(block * LANES, (block + 1) * LANES)
        value = sum_ref[rows, :]
        norm = jnp.sum(jnp.where(same, value[:, rows], 0.0), 1, keepdims=True)
        inv = jnp.broadcast_to(lax.rsqrt(norm / width + EPS), (LANES, LANES))
        high = inv.astype(BF16).astype(F32)
        inv = jnp.where(lane < LANES // 2, high, inv - high).astype(BF16)
        side, start = block * LANES // (vocab // 2), block * LANES % (vocab // 2)
        into = slice(below + start, below + start + LANES)
        left = side * (share + LANES)
        gram_ref[into, left : left + share] = mine[rows]
        gram_ref[into, left + share : left + share + LANES] = inv
        for part in range(3):
            high = value.astype(BF16)
            into = slice(part * vocab + block * LANES, part * vocab + (block + 1) * LANES)
            gram_ref[into, :] = high
            value = value - high.astype(F32)
            into = pl.ds(part * vocab + block * LANES, LANES)
            sem = out_sems.at[1 + block * 3 + part]
            outs.append(pltpu.make_async_copy(gram_ref.at[into], gram_hbm.at[into], sem))
            outs[-1].start()
    into = pl.ds(below, vocab // 2)
    outs.append(pltpu.make_async_copy(gram_ref.at[into], gram_hbm.at[into], out_sems.at[out_sems.shape[0] - 1]))
    outs[-1].start()
    for copy in outs:
        copy.wait()


def own_kernel(ids_ref, embed_ref, grad_ref, own_ref):
    vocab = embed_ref.shape[0]
    own_width = own_ref.shape[2]
    lanes = pl.ds(pl.multiple_of(lax.axis_index("path") * own_width, LANES), own_width)
    ids = ids_ref[...]
    columns = transposed(jnp.concatenate([joined(ids, kind) for kind in range(3)], 0))
    tok = jnp.broadcast_to(columns[:, 0:1], (LANES, LANES))
    place = jnp.broadcast_to(joined(ids, 1), (LANES, LANES))
    put = jnp.broadcast_to(joined(ids, 2), (LANES, LANES))
    first = lax.axis_index("ctx") * LANES
    subs = LANES // GROUP
    here = (place == (iota((LANES, LANES), 0) + first).astype(F32)) & (iota((LANES, LANES), 1) < subs)
    found = jnp.max(jnp.where(here, put, -1.0), 1, keepdims=True)
    base = jnp.where(found >= 0.0, found, tok)
    hots = jnp.concatenate([hot(tok, vocab), hot(base, vocab)], 0)
    both = dot(hots, embed_ref[:, lanes]).astype(BF16)
    own_ref[0] = both[:LANES]
    own_ref[1] = both[LANES:]


def multiply_rows(found, spec_ref, prod_ref, points, kind):
    _, quarter, share = spec_ref.shape
    for start in range(0, quarter, CHUNK):
        here = slice(start, start + CHUNK)
        after = slice(quarter + start, quarter + start + CHUNK)
        filt = [(spec_ref[2 * part, here, :], spec_ref[2 * part + 1, here, :]) for part in range(RADIX)]
        for point in range(points):
            lanes = slice(point * share, (point + 1) * share)
            values = butterfly([(value[here, lanes], value[after, lanes]) for value in found], -1)
            prods = []
            for (real, imag), (filt_real, filt_imag) in zip(values, filt):
                if kind == 1:
                    prods.append((real * filt_real + imag * filt_imag, imag * filt_real - real * filt_imag))
                else:
                    prods.append((real * filt_real - imag * filt_imag, imag * filt_real + real * filt_imag))
            lanes = slice((kind * points + point) * share, (kind * points + point + 1) * share)
            for part, (real, imag) in enumerate(butterfly(prods, 1)):
                prod_ref[part, here, lanes] = real.astype(BF16)
                prod_ref[part, after, lanes] = imag.astype(BF16)


def ids_kernel(vocab, msg_ref, hot_ref, subs_ref, put_ref):
    length = hot_ref.shape[0]
    quarter = length // RADIX
    n_ctx = msg_ref.shape[0]
    block_part = LANES // RADIX
    per_block = LANES // GROUP
    subs = n_ctx * per_block
    blocks = [msg_ref[block, LANES:, :].astype(F32) for block in range(n_ctx)]
    toks = transposed(jnp.concatenate([joined(block, 0) for block in blocks], 0))
    spread = sum(
        blocks[block] if block == 0 else pltpu.roll(blocks[block], block * per_block, 1)
        for block in range(n_ctx)
    )
    place = joined(spread, 1)
    put = joined(spread, 2)
    back = jnp.floor(place * (1.0 / RADIX))
    place = back + (place - RADIX * back) * quarter
    columns = transposed(jnp.concatenate([place, put], 0))
    for block in range(n_ctx):
        column = jnp.broadcast_to(toks[:, block : block + 1], (LANES, LANES))
        rows = hot(column, vocab)
        for side in range(RADIX):
            first = side * quarter + block * block_part
            hot_ref[first : first + block_part, :] = rows[side * block_part : (side + 1) * block_part]
    subs_ref[subs:, :] = hot(jnp.broadcast_to(columns[:, 1:2], (subs, LANES)), vocab)
    pick = jnp.concatenate(
        [
            (columns[:, 0:1] == (iota((subs, LANES), 1) + part * LANES).astype(F32)).astype(F32).astype(BF16)
            for part in range(length // LANES)
        ],
        1,
    )
    for index in range(length // LANES):
        row = (iota((LANES, subs), 0) + index * LANES).astype(F32)
        here = (row == place[:, :subs]).astype(F32).astype(BF16)
        put_ref[index * LANES : (index + 1) * LANES, :] = jnp.concatenate([here, here], 1)
    subs_ref[:subs, :] = dot(pick, hot_ref[...]).astype(BF16)


def feature_kernel(
    points, msg_ref, hot_ref, subs_hot_ref, put_ref, gram_ref, taps_ref, gain_ref, embed_hbm,
    signal_ref, k_ref, v_ref, inv_ref, pair_ref,
    embed_ref, sums_ref, found_ref, look_ref, subs_ref, sem,
):
    length = signal_ref.shape[0]
    quarter = length // RADIX
    vocab, width = embed_hbm.shape
    share = pair_ref.shape[2]
    subs = subs_hot_ref.shape[0] // 2
    first = (lax.axis_index("ctx") * points + lax.axis_index("path")) * share
    first = pl.multiple_of(first, LANES)
    below = 3 * vocab
    table = jnp.concatenate(
        [gram_ref[below:, : share + LANES], gram_ref[below:, share + LANES :]], 0
    )

    for index in range(length // LOOK_ROWS):
        rows = pl.ds(index * LOOK_ROWS, LOOK_ROWS)
        look_ref[rows, :] = dot(hot_ref[rows, :], table)

    alphas = [(point + 0.5) / points for point in range(points)]
    hots = subs_hot_ref[...]
    found = dot(jnp.concatenate([hots] * 3, 1), gram_ref[:below, :])
    hot_tok32, hot_base32 = hots[:subs].astype(F32), hots[subs:].astype(F32)
    tok_tok = jnp.sum(found[:subs] * hot_tok32, 1, keepdims=True)
    tok_base = jnp.sum(found[:subs] * hot_base32, 1, keepdims=True)
    base_tok = jnp.sum(found[subs:] * hot_tok32, 1, keepdims=True)
    tok_base = jnp.where(tok_base == 0.0, base_tok, tok_base)
    base_base = jnp.sum(found[subs:] * hot_base32, 1, keepdims=True)
    cancels = jnp.zeros((subs, 1), F32)
    for point in range(points):
        alpha = alphas[point]
        terms = (1.0 - alpha) ** 2 * base_base + alpha**2 * tok_tok
        total = terms + 2.0 * alpha * (1.0 - alpha) * tok_base
        cancels = jnp.maximum(cancels, (total < CANCEL * terms).astype(F32))
        inv = lax.rsqrt(jnp.maximum(total, 0.0) / width + EPS)
        sums_ref[point] = jnp.broadcast_to(inv, (subs, LANES))

    @pl.when(jnp.max(cancels) > 0.5)
    def _():
        sums_ref[...] = jnp.zeros_like(sums_ref)
        wide = found_ref.shape[1]

        @pl.loop(0, width // wide)
        def _(step):
            lanes = pl.ds(pl.multiple_of(step * wide, wide), wide)
            copy = pltpu.make_async_copy(embed_hbm.at[:, lanes], embed_ref, sem)
            copy.start()
            copy.wait()
            found_ref[...] = dot(hots, embed_ref[...])
            for block in range(subs // GROUP):
                rows = slice(block * GROUP, (block + 1) * GROUP)
                sums = [sums_ref[point, rows, :] for point in range(points)]
                for column in range(wide // LANES):
                    cut = slice(column * LANES, (column + 1) * LANES)
                    base = found_ref[subs + block * GROUP : subs + (block + 1) * GROUP, cut]
                    diff = found_ref[rows, cut] - base
                    for point in range(points):
                        value = base + alphas[point] * diff
                        sums[point] = sums[point] + value * value
                for point in range(points):
                    sums_ref[point, rows, :] = sums[point]

        for point in range(points):
            mean = jnp.sum(sums_ref[point], 1, keepdims=True) / width
            sums_ref[point] = jnp.broadcast_to(lax.rsqrt(mean + EPS), (subs, LANES))

    high = [dot(hots[subs:], table[:, :share]), jnp.ones((subs, LANES), F32)]
    low = [jnp.zeros((subs, LANES), F32)] * 2
    for point in range(points):
        inv = sums_ref[point]
        high.append(inv.astype(BF16).astype(F32))
        low.append(inv - high[-1])
    held = jnp.concatenate([jnp.concatenate(high, 1), jnp.concatenate(low, 1)], 0).astype(BF16)
    for index in range(length // LOOK_ROWS):
        rows = pl.ds(index * LOOK_ROWS, LOOK_ROWS)
        subs_ref[rows, :] = dot(put_ref[rows, :], held)

    cols = points * share
    block_part = LANES // RADIX
    last = {side: [jnp.zeros((GROUP, share), F32)] * points for side in (RADIX - 2, RADIX - 1)}
    gain = gain_ref[:, pl.ds(first, share)]
    taps = [taps_ref[f, :, pl.ds(first, share)].astype(F32) for f in range(3)]
    taps = [[taps[f][tap : tap + 1] for tap in range(3)] for f in range(3)]

    for start in range(0, quarter, CHUNK):
        block, inside = start // block_part, start % block_part
        sides = []
        for side in range(RADIX):
            rows = pl.ds(side * quarter + start, CHUNK)
            tok = look_ref[rows, :share]
            inv = look_ref[rows, share:]
            inv = inv + pltpu.roll(inv, LANES // 2, 1)
            chosen = subs_ref[rows, share : 2 * share] > 0.5
            base = jnp.where(chosen, subs_ref[rows, :share], tok)
            pair_ref[0, rows, :] = tok.astype(BF16)
            pair_ref[1, rows, :] = base.astype(BF16)
            sent = pl.ds(side * block_part + inside, CHUNK)
            upstream = msg_ref[block, sent, :].astype(F32)
            sides.append((rows, gain * base, gain * (tok - base), inv, chosen, upstream))
        for point in range(points):
            lanes = slice(point * share, (point + 1) * share)
            recent = []
            for rows, base, diff, inv_tok, chosen, _ in sides:
                inv = jnp.where(
                    chosen, subs_ref[rows, (2 + point) * share : (3 + point) * share], inv_tok
                )
                inv_ref[rows, lanes] = inv
                recent.append(rounded((base + alphas[point] * diff) * inv))
            backs = []
            for side in (RADIX - 2, RADIX - 1):
                window = jnp.concatenate([last[side][point], recent[side]], 0)
                last[side][point] = recent[side][CHUNK - GROUP :]
                backs.append(window[GROUP - 1 : GROUP - 1 + CHUNK])
            recent = backs + recent
            for side in range(RADIX):
                rows, upstream = sides[side][0], sides[side][5]
                feats = [sum(taps[f][tap] * recent[side + 2 - tap] for tap in range(3)) for f in range(3)]
                k_ref[rows, lanes] = feats[1]
                v_ref[rows, lanes] = feats[2]
                signal_ref[rows, lanes] = (feats[1] * feats[2]).astype(BF16)
                after = slice(cols + point * share, cols + (point + 1) * share)
                signal_ref[rows, after] = (upstream * feats[0]).astype(BF16)


def gradient_kernel(
    points, width, msg_ref, pair_ref, taps_ref, gain_ref,
    signal_ref, k_ref, v_ref, inv_ref, table_ref, back_ref, spec_ref,
    grad_ref,
    prod_ref,
):
    _, quarter, share = spec_ref.shape
    cols = points * share
    n_ctx = msg_ref.shape[0]
    block_part = LANES // RADIX
    first = (lax.axis_index("ctx") * points + lax.axis_index("path")) * share
    first = pl.multiple_of(first, LANES)
    gain = gain_ref[:, pl.ds(first, share)]
    taps = [taps_ref[f, :, pl.ds(first, share)].astype(F32) for f in range(3)]
    taps = [[taps[f][tap : tap + 1] for tap in range(3)] for f in range(3)]

    found = []
    for kind in range(2):
        signal = slice(kind * cols, (kind + 1) * cols)
        spectra = [
            dot(table_ref[side], signal_ref[side * quarter : (side + 1) * quarter, signal])
            for side in range(RADIX)
        ]
        multiply_rows(spectra, spec_ref, prod_ref, points, kind)
    for kind in range(2):
        signal = slice(kind * cols, (kind + 1) * cols)
        found.append([dot(back_ref[side], prod_ref[side, :, signal]) for side in range(RADIX)])

    carried = [[jnp.zeros((GROUP, share), F32)] * points for _ in range(3)]
    lane, row = iota((GROUP, LANES), 1), iota((GROUP, LANES), 0)
    for start in reversed(range(0, quarter, CHUNK)):
        block, inside = start // block_part, start % block_part
        if inside + CHUNK == block_part:
            means = [jnp.zeros((GROUP, LANES), F32)] * 2
        kept = [{} for _ in range(RADIX)]
        for offset in reversed(range(0, CHUNK, GROUP)):
            here = slice(start + offset, start + offset + GROUP)
            sides = []
            for side in range(RADIX):
                rows = slice(side * quarter + start + offset, side * quarter + start + offset + GROUP)
                sent = pl.ds(side * block_part + inside, CHUNK)
                upstream = msg_ref[block, sent, :].astype(F32)[offset : offset + GROUP]
                sides.append([rows, upstream] + [jnp.zeros((GROUP, share), F32)] * 4)
            for point in reversed(range(points)):
                lanes = slice(point * share, (point + 1) * share)
                by_tap = []
                for side in range(RADIX):
                    rows, upstream = sides[side][:2]
                    grad_z = found[1][side][here, lanes]
                    grads = (
                        upstream * found[0][side][here, lanes],
                        grad_z * v_ref[rows, lanes],
                        grad_z * k_ref[rows, lanes],
                    )
                    by_tap.append([sum(taps[f][tap] * grads[f] for f in range(3)) for tap in range(3)])
                ahead = []
                for slot, value in enumerate((by_tap[0][1], by_tap[0][2], by_tap[1][2])):
                    window = jnp.concatenate([value, carried[slot][point]], 0)
                    carried[slot][point] = value
                    ahead.append(window[1 : 1 + GROUP])
                by_tap += [[None, ahead[0], ahead[1]], [None, None, ahead[2]]]
                for side in range(RADIX):
                    rows, _, total, sum0, sum1, sum2 = sides[side]
                    inv = inv_ref[rows, lanes]
                    along = inv * (by_tap[side][0] + by_tap[side + 1][1] + by_tap[side + 2][2])
                    total = total + along
                    sum0 = sum0 + along * (inv * inv)
                    sum1 = sum1 + sum0
                    sides[side][2:] = [total, sum0, sum1, sum2 + sum1]
            for side in range(RADIX):
                _, _, total, sum0, sum1, sum2 = sides[side]
                rows = pl.ds(side * quarter + start, CHUNK)
                base = pair_ref[1, rows, :].astype(F32)[offset : offset + GROUP]
                diff = pair_ref[0, rows, :].astype(F32)[offset : offset + GROUP] - base
                once = (sum1 - 0.5 * sum0) * (1.0 / points)
                twice = (2.0 * (sum2 - sum1) + 0.25 * sum0) * (1.0 / points**2)
                to_tok = base * once + diff * twice
                to_base = base * sum0 + diff * once - to_tok
                kept[side][offset] = gain * total
                for kind, value in enumerate((gain * to_tok, gain * to_base)):
                    value = jnp.sum(value, 1, keepdims=True)
                    at = lane == row + (side * block_part + inside + offset)
                    means[kind] = means[kind] + jnp.where(at, value, 0.0)
        for side in range(RADIX):
            total = jnp.concatenate([kept[side][offset] for offset in range(0, CHUNK, GROUP)], 0)
            grad_ref[block, pl.ds(side * block_part + inside, CHUNK), :] = total.astype(BF16)
        if inside == 0:
            sent = []
            for value in means:
                value = jnp.sum(value, 0, keepdims=True) / width
                high = value.astype(BF16).astype(F32)
                sent += [high, value - high]
            sent.append(jnp.zeros((grad_ref.shape[1] - LANES - len(sent), LANES), F32))
            grad_ref[block, LANES:, :] = jnp.concatenate(sent, 0).astype(BF16)


def partial_kernel(grad_ref, *out_refs):
    rows, _ = out_refs[0].shape
    n_ctx = grad_ref.shape[0]
    each = n_ctx // len(out_refs)
    spare = sum(grad_ref[block, LANES:, :].astype(F32) for block in range(n_ctx))
    sums = [spare[0:1] + spare[1:2], spare[2:3] + spare[3:4]]
    sent = []
    for value in sums:
        high = value.astype(BF16).astype(F32)
        sent += [high, value - high]
    sent.append(jnp.zeros((rows - each * LANES - len(sent), LANES), F32))
    sent = jnp.concatenate(sent, 0).astype(BF16)
    path = lax.axis_index("path")
    for step, ref in enumerate(out_refs):
        dest = path ^ step
        for piece in range(each):
            ref[piece * LANES : (piece + 1) * LANES, :] = grad_ref[dest * each + piece, :LANES, :]
        ref[each * LANES :, :] = sent


def finish_kernel(own_ref, *refs):
    grad_refs, (path_hbm, attr_hbm, path_ref, attr_ref, sems) = refs[:-5], refs[-5:]
    points = len(grad_refs)
    rows, share = grad_refs[0].shape
    pieces = rows // LANES
    spare = sum(ref[pieces * LANES :, :].astype(F32) for ref in grad_refs)
    lane = iota((LANES, LANES), 1)
    part = LANES // RADIX
    order = (iota((LANES, LANES), 0) == RADIX * (lane % part) + lane // part).astype(F32).astype(BF16)
    left, split = jnp.concatenate([spare[0:1] + spare[1:2], spare[2:3] + spare[3:4]], 0), []
    for _ in range(3):
        split.append(left.astype(BF16).astype(F32))
        left = left - split[-1]
    split = jnp.concatenate(split + [jnp.zeros((2, LANES), F32)], 0).astype(BF16)
    columns = lax.dot_general(order, split, (((1,), (1,)), ((), ())), preferred_element_type=F32)
    to_tok = columns[:, 0:1] + columns[:, 2:3] + columns[:, 4:5]
    to_base = columns[:, 1:2] + columns[:, 3:4] + columns[:, 5:6]
    path = lax.axis_index("path")
    copies = []
    for step, ref in enumerate(grad_refs):
        for piece in range(pieces):
            slot = step * pieces + piece
            first = (piece * points + (path ^ step)) * share
            lanes = pl.ds(pl.multiple_of(first, LANES), share)
            tok = own_ref[0, :, lanes].astype(F32)
            base = own_ref[1, :, lanes].astype(F32)
            grad = dot(order, ref[piece * LANES : (piece + 1) * LANES, :])
            grad = (grad - tok * to_tok - base * to_base) / points
            path_ref[slot] = grad
            attr_ref[slot] = (tok - base) * grad
            for kind, (source, target) in enumerate(((path_ref, path_hbm), (attr_ref, attr_hbm))):
                copies.append(
                    pltpu.make_async_copy(source.at[slot], target.at[:, lanes], sems.at[kind, slot])
                )
                copies[-1].start()
    for copy in copies:
        copy.wait()


def any_spec():
    return pl.BlockSpec(memory_space=pl.ANY)


def vmem_spec():
    return pl.BlockSpec(memory_space=pltpu.VMEM)


def hbm_spec():
    return pl.BlockSpec(memory_space=pltpu.HBM)


def call(kernel, ins, outs, scratch, flops, moved, mebibytes):
    return pl.pallas_call(
        kernel,
        in_specs=ins,
        out_specs=[spec for spec, _ in outs],
        out_shape=[shape for _, shape in outs],
        scratch_shapes=scratch,
        compiler_params=pltpu.CompilerParams(vmem_limit_bytes=mebibytes * 2**20),
        cost_estimate=pl.CostEstimate(flops=flops, bytes_accessed=moved, transcendentals=0),
    )


def shape(dims, dtype):
    return jax.ShapeDtypeStruct(dims, dtype)


def kernel_body(tokens, sub_pos, sub_base, embed, norm_gain, fir_taps, long_filter, skip_gain, cotangent):
    n_path, n_ctx = lax.axis_size("path"), lax.axis_size("ctx")
    points = n_path
    tok_rows = tokens.shape[0]
    length = tok_rows * n_ctx
    vocab, width = embed.shape
    share = width // (n_path * n_ctx)
    subs = sub_pos.shape[0] * n_ctx
    own_width = width // n_path
    cols = points * share
    quarter = length // RADIX
    tables = dft_tables(length)
    dma = pltpu.SemaphoreType.DMA
    transform_flops = length * length
    spare = 8

    msg, ids = call(
        pack_kernel,
        [hbm_spec()] * 4,
        [
            (vmem_spec(), shape((n_ctx, tok_rows + spare, share), BF16)),
            (vmem_spec(), shape((spare, LANES), F32)),
        ],
        [
            pltpu.VMEM((1, tok_rows), jnp.int32),
            pltpu.VMEM((1, sub_pos.shape[0]), jnp.int32),
            pltpu.VMEM((1, sub_pos.shape[0]), jnp.int32),
            pltpu.VMEM((tok_rows, n_ctx * share), BF16),
            dma((n_ctx + 3,)),
        ],
        length * share,
        8 * length * share,
        60,
    )(
        tokens.reshape(1, tok_rows),
        sub_pos.reshape(1, -1),
        sub_base.reshape(1, -1),
        cotangent,
    )
    msg = lax.all_to_all(msg, "ctx", 0, 0, tiled=True)

    gain = norm_gain.reshape(1, width)
    skip = skip_gain.reshape(1, n_path * share)
    spec, gram = call(
        prepare_kernel,
        [hbm_spec()] * 4 + [any_spec()],
        [
            (any_spec(), shape((2 * RADIX, quarter, share), F32)),
            (any_spec(), shape((3 * vocab + vocab // 2, vocab), BF16)),
        ],
        [
            pltpu.VMEM((length, share), F32),
            pltpu.VMEM((RADIX, 2 * quarter, quarter), BF16),
            pltpu.VMEM((vocab, width), BF16),
            pltpu.VMEM((1, share), F32),
            pltpu.VMEM((vocab, vocab), F32),
            pltpu.VMEM((2 * RADIX, quarter, share), F32),
            pltpu.VMEM((3 * vocab + vocab // 2, vocab), BF16),
            dma((7,)),
            dma((3 * vocab // LANES + 2,)),
        ],
        2 * vocab * vocab * width,
        2 * vocab * width,
        58,
    )(long_filter, tables[0], embed, skip, ids)

    hots, subs_hots, put_hots = call(
        functools.partial(ids_kernel, vocab),
        [vmem_spec()],
        [
            (vmem_spec(), shape((length, vocab), BF16)),
            (vmem_spec(), shape((2 * subs, vocab), BF16)),
            (vmem_spec(), shape((length, 2 * subs), BF16)),
        ],
        [],
        2 * 10**9,
        4 * 10**6,
        8,
    )(msg)
    wide = 4 * LANES
    signal, k_feat, v_feat, inv, pair = call(
        functools.partial(feature_kernel, points),
        [vmem_spec()] * 7 + [hbm_spec()],
        [(vmem_spec(), shape((length, 2 * cols), BF16))]
        + [(vmem_spec(), shape((length, cols), F32))] * 3
        + [(vmem_spec(), shape((2, length, share), BF16))],
        [
            pltpu.VMEM((vocab, wide), BF16),
            pltpu.VMEM((points, subs, LANES), F32),
            pltpu.VMEM((2 * subs, wide), F32),
            pltpu.VMEM((length, 2 * share), F32),
            pltpu.VMEM((length, (2 + points) * share), F32),
            dma,
        ],
        2 * length * vocab * 3 * share,
        2 * vocab * width + 16 * length * cols,
        39,
    )(msg, hots, subs_hots, put_hots, gram, fir_taps, gain, embed)

    grad = call(
        functools.partial(gradient_kernel, points, width),
        [vmem_spec()] * 11,
        [(vmem_spec(), shape((n_ctx, tok_rows + spare, share), BF16))],
        [
            pltpu.VMEM((RADIX, 2 * quarter, 2 * cols), BF16),
        ],
        4 * transform_flops * cols,
        4 * length * length + 16 * length * cols,
        32,
    )(msg, pair, fir_taps, gain, signal, k_feat, v_feat, inv, *tables, spec)[0]

    own = call(
        own_kernel,
        [vmem_spec(), vmem_spec(), any_spec()],
        [(vmem_spec(), shape((2, tok_rows, own_width), BF16))],
        [],
        4 * tok_rows * vocab * own_width,
        2 * vocab * own_width,
        10,
    )(ids, embed, grad)[0]
    grad = lax.all_to_all(grad, "ctx", 0, 0, tiled=True)
    each = n_ctx // n_path
    parts = call(
        partial_kernel,
        [vmem_spec()],
        [(vmem_spec(), shape((each * tok_rows + spare, share), BF16))] * n_path,
        [],
        spare * LANES * n_ctx,
        4 * length * share,
        4,
    )(grad)
    parts = [
        part if step == 0 else lax.ppermute(part, "path", [(p, p ^ step) for p in range(n_path)])
        for step, part in enumerate(parts)
    ]
    out = shape((tok_rows, own_width), F32)
    return tuple(
        call(
            finish_kernel,
            [vmem_spec()] * (1 + n_path),
            [(any_spec(), out), (any_spec(), out)],
            [pltpu.VMEM((n_path * each, tok_rows, share), F32)] * 2 + [dma((2, n_path * each))],
            8 * tok_rows * own_width,
            14 * tok_rows * own_width,
            8,
        )(own, *parts)
    )


def plain_body(tokens, sub_pos, sub_base, embed, norm_gain, fir_taps, long_filter, skip_gain, cotangent):
    n_path, n_ctx = lax.axis_size("path"), lax.axis_size("ctx")
    path, ctx = lax.axis_index("path"), lax.axis_index("ctx")
    points = n_path
    tok_rows = tokens.shape[0]
    length = tok_rows * n_ctx
    width = embed.shape[1]
    share = width // (n_path * n_ctx)
    own_width = width // n_path
    first = (ctx * n_path + path) * share
    alphas = ((jnp.arange(points, dtype=jnp.int32)).astype(F32) + 0.5) / points
    alphas = alphas[:, None, None]

    local = jnp.arange(tok_rows, dtype=jnp.int32)[:, None] + ctx * tok_rows == sub_pos[None, :]
    put = jnp.sum(jnp.where(local, sub_base[None, :], 0), 1)
    base_ids = jnp.where(jnp.any(local, 1), put, tokens)
    rows_tok = jnp.take(embed, tokens, axis=0).astype(F32)
    rows_base = jnp.take(embed, base_ids, axis=0).astype(F32)
    rows_in = rows_base[None] + alphas * (rows_tok - rows_base)[None]
    inv = lax.rsqrt(jnp.mean(rows_in * rows_in, -1) + EPS)
    inv = lax.all_gather(inv, "ctx", axis=1, tiled=True)[:, :, None]
    all_tok = lax.all_gather(tokens, "ctx", tiled=True)
    all_base = lax.all_gather(base_ids, "ctx", tiled=True)

    cot = cotangent.reshape(tok_rows, n_ctx, n_path, share)
    cot = lax.dynamic_index_in_dim(cot, path, 2, keepdims=False)
    cot = lax.all_to_all(cot.transpose(1, 0, 2), "ctx", 0, 0, tiled=True)
    upstream = cot.reshape(1, length, share).astype(F32)
    mine = lax.dynamic_slice_in_dim(embed, first, share, 1)
    gain = lax.dynamic_slice_in_dim(norm_gain, first, share, 0)
    taps = lax.dynamic_slice_in_dim(fir_taps, first, share, 2).astype(F32)
    filt = lax.dynamic_slice_in_dim(long_filter, path * share, share, 1)
    skip = lax.dynamic_slice_in_dim(skip_gain, path * share, share, 0)

    emb_tok = jnp.take(mine, all_tok, axis=0).astype(F32)
    emb_base = jnp.take(mine, all_base, axis=0).astype(F32)
    inputs = emb_base[None] + alphas * (emb_tok - emb_base)[None]
    normed = rounded(inputs * inv * gain)
    q_feat, k_feat, v_feat = (
        taps[f, 0] * normed + taps[f, 1] * shifted(normed, 1) + taps[f, 2] * shifted(normed, 2)
        for f in range(3)
    )
    filter_spec = spectrum(filt[None])
    conv = rounded(long_conv(rounded(k_feat * v_feat), filter_spec, skip, False))
    grad_z = rounded(long_conv(rounded(upstream * q_feat), filter_spec, skip, True))
    grads = (rounded(upstream * conv), rounded(grad_z * v_feat), rounded(grad_z * k_feat))
    by_tap = [sum(taps[f, tap] * grads[f] for f in range(3)) for tap in range(3)]
    scaled = gain * (by_tap[0] + shifted(by_tap[1], -1) + shifted(by_tap[2], -2))
    grad = jnp.sum(inv * scaled, 0).astype(BF16)
    along = jnp.sum(inputs * scaled, -1, keepdims=True) * inv**3 / width
    part = jnp.stack([jnp.sum(alphas * along, 0)[:, 0], jnp.sum((1.0 - alphas) * along, 0)[:, 0]])
    part = lax.psum(part, ("path", "ctx"))
    part = lax.dynamic_slice_in_dim(part, ctx * tok_rows, tok_rows, 1)

    back = lax.all_to_all(grad.reshape(n_ctx, tok_rows, share), "ctx", 0, 0, tiled=True)
    back = back.reshape(n_path, n_ctx // n_path, tok_rows, share)
    back = lax.all_to_all(back, "path", 0, 0, tiled=True).astype(F32)
    back = back.transpose(2, 1, 0, 3).reshape(tok_rows, own_width)
    own_tok = lax.dynamic_slice_in_dim(rows_tok, path * own_width, own_width, 1)
    own_base = lax.dynamic_slice_in_dim(rows_base, path * own_width, own_width, 1)
    grad = (back - own_tok * part[0][:, None] - own_base * part[1][:, None]) / points
    return (grad, (own_tok - own_base) * grad)


def body(tokens, sub_pos, sub_base, embed, *rest):
    n_path, n_ctx = lax.axis_size("path"), lax.axis_size("ctx")
    tok_rows = tokens.shape[0]
    share = embed.shape[1] // (n_path * n_ctx)
    tables = 2 * (tok_rows * n_ctx) ** 2
    fits = share == LANES and tok_rows == LANES and n_ctx == GROUP and tables <= TABLE_BYTES
    fits = fits and n_ctx % n_path == 0 and n_path & (n_path - 1) == 0
    chosen = kernel_body if fits else plain_body
    return chosen(tokens, sub_pos, sub_base, embed, *rest)


def solution(mesh):
    return jax.shard_map(
        body,
        mesh=mesh,
        in_specs=(
            P("ctx"),
            P("ctx"),
            P("ctx"),
            P(),
            P(),
            P(),
            P(None, "ctx"),
            P("ctx"),
            P("ctx", None),
        ),
        out_specs=(P("ctx", "path"), P("ctx", "path")),
        check_vma=False,
    )
```

profile of v0, /device:TPU:0, one launch (start us, length us, event | category | flops | bytes accessed | tf_op | source)
XLA Modules:
  0.0 51.4 jit_solution(11820460266108466340)
XLA Ops:
  0.6 2.0 %shard_map.122 = (bf16[8,136,128]{2,1,0:T(8,128)(2,1)}, f32[8,128]{1,0:T(8,128)}) custom-call(s32[1,128]{1,0:T(1,128)} %bitcast.7, s32[1,16]{1,0:T(1,128)} %bitcast.8, s32[1,16]{1,0:T(1,128)} %bitcast.9, bf16[128,4096]{1,0:T(8,128)(2,1)} %cot_hbm.1), custom_call_target="tpu_custom_call" | custom-call | flops 131072 | bytes 1048576 | tf_op jit(solution)/shard_map/pallas_call | solution.py:717
  2.6 7.3 %all-to-all-start = ((bf16[8,136,128]{2,1,0:T(8,128)(2,1)}), bf16[8,136,128]{2,1,0:T(8,128)(2,1)S(1)}, u32[]{:S(2)}, u32[]{:S(2)}) async-start(bf16[8,136,128]{2,1,0:T(8,128)(2,1)} %get-tuple-element.19), calls=%async_computation | async-start | bytes 557056 | tf_op jit(solution)/shard_map/all_to_all | solution.py:740
  9.9 6.0 %shard_map.124 = (f32[8,256,128]{2,1,0:T(8,128)}, bf16[1792,512]{1,0:T(8,128)(2,1)}) custom-call(f32[1024,512]{1,0:T(8,128)} %filt_hbm.1, bf16[4,512,256]{2,1,0:T(8,128)(2,1)} %constant.4.clone.table_hbm.table_ref, bf16[512,4096]{1,0:T(8,128)(2,1)} %embed_ref.1, f32[1,512]{1,0:T(1,128)} %bitcast.10, f32[8,128]{1,0:T(8,128)} %get-tuple-element.18.after_ref.ids_ref), custom_call_target="tpu_custom_call" | custom-call | flops 2147483648 | bytes 4194304 | tf_op jit(solution)/shard_map/pallas_call | solution.py:744
  15.9 0.0 copy-start.1
  15.9 0.0 copy-start.5
  15.9 0.0 copy-start.6
  15.9 3.3 %all-to-all-done.msg_ref = bf16[8,136,128]{2,1,0:T(8,128)(2,1)S(1)} async-done(((bf16[8,136,128]{2,1,0:T(8,128)(2,1)}), bf16[8,136,128]{2,1,0:T(8,128)(2,1)S(1)}, u32[]{:S(2)}, u32[]{:S(2)}) %all-to-all-start) | async-done | bytes 278560 | tf_op jit(solution)/shard_map/all_to_all | solution.py:740
  19.2 0.7 %shard_map.123 = (bf16[1024,512]{1,0:T(8,128)(2,1)S(1)}, bf16[256,512]{1,0:T(8,128)(2,1)S(1)}, bf16[1024,256]{1,0:T(8,128)(2,1)S(1)}) custom-call(bf16[8,136,128]{2,1,0:T(8,128)(2,1)S(1)} %all-to-all-done.msg_ref), custom_call_target="tpu_custom_call" | custom-call | flops 2000000000 | bytes 4000000 | tf_op jit(solution)/shard_map/pallas_call | solution.py:767
  19.9 0.0 copy-done.1
  19.9 0.0 copy-done.5
  19.9 0.0 copy-done.6
  19.9 0.0 copy-start.2
  19.9 0.0 copy-start.3
  19.9 0.0 copy-start.4
  19.9 4.1 %shard_map.125 = (bf16[1024,1024]{1,0:T(8,128)(2,1)S(1)}, f32[1024,512]{1,0:T(8,128)S(1)}, f32[1024,512]{1,0:T(8,128)S(1)}, f32[1024,512]{1,0:T(8,128)S(1)}, bf16[2,1024,128]{2,1,0:T(8,128)(2,1)S(1)}) custom-call(bf16[8,136,128]{2,1,0:T(8,128)(2,1)S(1)} %all-to-all-done.msg_ref, bf16[1024,512]{1,0:T(8,128)(2,1)S(1)} %get-tuple-element.20.hot_ref, ...), custom_call_target="tpu_custom_call" | custom-call | flops 402653184 | bytes 12582912 | tf_op jit(solution)/shard_map/pallas_call | solution.py:781
  24.1 0.0 copy-done.2
  24.1 0.0 copy-done.3
  24.1 0.0 copy-done.4
  24.1 0.0 copy-start
  24.1 0.0 copy-start.7
  24.1 6.6 %shard_map.126.grad_ref = bf16[8,136,128]{2,1,0:T(8,128)(2,1)S(1)} custom-call(bf16[8,136,128]{2,1,0:T(8,128)(2,1)S(1)} %all-to-all-done.msg_ref, bf16[2,1024,128]{2,1,0:T(8,128)(2,1)S(1)} %get-tuple-element.24.pair_ref, bf16[3,3,4096]{2,1,0:T(4,128)(2,1)S(1)} %copy-done.5, f32[1,4096]{1,0:T(1,128)S(1)} %bitcast.6, ...), custom_call_target="tpu_custom_call" | custom-call | flops 2147483648 | bytes 12582912 | tf_op jit(solution)/shard_map/pallas_call | solution.py:800
  30.8 13.1 %all_to_all.10.grad_ref = bf16[8,136,128]{2,1,0:T(8,128)(2,1)S(1)} all-to-all(bf16[8,136,128]{2,1,0:T(8,128)(2,1)S(1)} %shard_map.126.grad_ref), channel_id=1, replica_groups=mesh['path'=4,'ctx'=8] {'ctx'}, dimensions={0} | all-to-all | bytes 557056 | tf_op jit(solution)/shard_map/all_to_all | solution.py:821
  43.9 0.1 collective-permute-start
  44.0 1.6 %collective-permute-start.1 = (bf16[264,128]{1,0:T(8,128)(2,1)S(1)}, bf16[264,128]{1,0:T(8,128)(2,1)S(1)}, u32[]{:S(2)}, u32[]{:S(2)}) collective-permute-start(bf16[264,128]{1,0:T(8,128)(2,1)S(1)} %get-tuple-element.32), channel_id=1, source_target_pairs={{0,16},{8,24},{16,0},{24,8},{1,17},{9,25},{17,1},{25,9},{2,18},{10... | collective-permute-start | bytes 202760 | tf_op jit(solution)/shard_map/ppermute | solution.py:833
  45.5 0.3 collective-permute-start.2
  45.8 0.0 copy-done
  45.8 0.0 copy-done.7
  45.8 0.6 %shard_map.127.own_ref = bf16[2,128,1024]{2,1,0:T(8,128)(2,1)S(1)} custom-call(f32[8,128]{1,0:T(8,128)S(1)} %copy-done.7, bf16[512,4096]{1,0:T(8,128)(2,1)S(1)} %copy-done, bf16[8,136,128]{2,1,0:T(8,128)(2,1)S(1)} %shard_map.126.grad_ref), custom_call_target="tpu_custom_call" | custom-call | flops 268435456 | bytes 1048576 | tf_op jit(solution)/shard_map/pallas_call | solution.py:812
  46.4 0.0 collective-permute-done.refs_1_
  46.4 2.1 %collective-permute-done.1.refs_2_ = bf16[264,128]{1,0:T(8,128)(2,1)S(1)} collective-permute-done((bf16[264,128]{1,0:T(8,128)(2,1)S(1)}, bf16[264,128]{1,0:T(8,128)(2,1)S(1)}, u32[]{:S(2)}, u32[]{:S(2)}) %collective-permute-start.1) | collective-permute-done | bytes 67616 | tf_op jit(solution)/shard_map/ppermute | solution.py:833
  48.6 1.1 %collective-permute-done.2.refs_3_ = bf16[264,128]{1,0:T(8,128)(2,1)S(1)} collective-permute-done((bf16[264,128]{1,0:T(8,128)(2,1)S(1)}, bf16[264,128]{1,0:T(8,128)(2,1)S(1)}, u32[]{:S(2)}, u32[]{:S(2)}) %collective-permute-start.2) | collective-permute-done | bytes 67616 | tf_op jit(solution)/shard_map/ppermute | solution.py:833
  49.6 1.6 %shard_map.129 = (f32[128,1024]{1,0:T(8,128)}, f32[128,1024]{1,0:T(8,128)}) custom-call(bf16[2,128,1024]{2,1,0:T(8,128)(2,1)S(1)} %shard_map.127.own_ref, bf16[264,128]{1,0:T(8,128)(2,1)S(1)} %get-tuple-element.30.refs_0_, bf16[264,128]{1,0:T(8,128)(2,1)S(1)} %collective-permute-done.refs_1_, bf16[264,128]{1,0:T(8,128)(2,1)S(1)} %collective-permute-done.1.refs_2_, ...), custom_call_target="tpu_custom_call" | custom-call | flops 1048576 | bytes 1835008 | tf_op jit(solution)/shard_map/pallas_call | solution.py:838
  (1 shorter events, 0.0 us)
Async XLA Ops:
  2.6 16.6 %all-to-all-start = ((bf16[8,136,128]{2,1,0:T(8,128)(2,1)}), bf16[8,136,128]{2,1,0:T(8,128)(2,1)S(1)}, u32[]{:S(2)}, u32[]{:S(2)}) async-start(bf16[8,136,128]{2,1,0:T(8,128)(2,1)} %get-tuple-element.19), calls=%async_computation | async-start | bytes 557056 | tf_op jit(solution)/shard_map/all_to_all | solution.py:740
  15.9 4.0 %copy-start.1 = (bf16[1792,512]{1,0:T(8,128)(2,1)S(1)}, bf16[1792,512]{1,0:T(8,128)(2,1)}, u32[]{:S(2)}) copy-start(bf16[1792,512]{1,0:T(8,128)(2,1)} %get-tuple-element.23.gram_ref) | copy-start | bytes 5505028
  15.9 4.0 %copy-start.5 = (bf16[3,3,4096]{2,1,0:T(4,128)(2,1)S(1)}, bf16[3,3,4096]{2,1,0:T(4,128)(2,1)}, u32[]{:S(2)}) copy-start(bf16[3,3,4096]{2,1,0:T(4,128)(2,1)} %taps_ref.3) | copy-start | bytes 221188
  15.9 4.0 %copy-start.6 = (f32[4096]{0:T(1024)S(1)}, f32[4096]{0:T(1024)}, u32[]{:S(2)}) copy-start(f32[4096]{0:T(1024)} %param.15) | copy-start | bytes 49156
  19.9 4.2 %copy-start.2 = (bf16[4,512,256]{2,1,0:T(8,128)(2,1)S(1)}, bf16[4,512,256]{2,1,0:T(8,128)(2,1)}, u32[]{:S(2)}) copy-start(bf16[4,512,256]{2,1,0:T(8,128)(2,1)} %constant.4.clone.table_hbm.table_ref) | copy-start | bytes 3145732
  19.9 4.2 %copy-start.3 = (bf16[4,256,512]{2,1,0:T(8,128)(2,1)S(1)}, bf16[4,256,512]{2,1,0:T(8,128)(2,1)}, u32[]{:S(2)}) copy-start(bf16[4,256,512]{2,1,0:T(8,128)(2,1)} %constant.5.clone.back_ref) | copy-start | bytes 3145732
  19.9 4.2 %copy-start.4 = (f32[8,256,128]{2,1,0:T(8,128)S(1)}, f32[8,256,128]{2,1,0:T(8,128)}, u32[]{:S(2)}) copy-start(f32[8,256,128]{2,1,0:T(8,128)} %get-tuple-element.29.spec_ref) | copy-start | bytes 3145732
  24.1 21.7 %copy-start = (bf16[512,4096]{1,0:T(8,128)(2,1)S(1)}, bf16[512,4096]{1,0:T(8,128)(2,1)}, u32[]{:S(2)}) copy-start(bf16[512,4096]{1,0:T(8,128)(2,1)} %embed_ref.1) | copy-start | bytes 12582916
  24.1 21.7 %copy-start.7 = (f32[8,128]{1,0:T(8,128)S(1)}, f32[8,128]{1,0:T(8,128)}, u32[]{:S(2)}) copy-start(f32[8,128]{1,0:T(8,128)} %get-tuple-element.18.after_ref.ids_ref) | copy-start | bytes 12292
  43.9 2.5 %collective-permute-start = (bf16[264,128]{1,0:T(8,128)(2,1)S(1)}, bf16[264,128]{1,0:T(8,128)(2,1)S(1)}, u32[]{:S(2)}, u32[]{:S(2)}) collective-permute-start(bf16[264,128]{1,0:T(8,128)(2,1)S(1)} %get-tuple-element.31), channel_id=1, source_target_pairs={{0,8},{8,0},{16,24},{24,16},{1,9},{9,1},{17,25},{25,17},{2,10},{10... | collective-permute-start | bytes 202760 | tf_op jit(solution)/shard_map/ppermute | solution.py:833
  44.0 4.6 %collective-permute-start.1 = (bf16[264,128]{1,0:T(8,128)(2,1)S(1)}, bf16[264,128]{1,0:T(8,128)(2,1)S(1)}, u32[]{:S(2)}, u32[]{:S(2)}) collective-permute-start(bf16[264,128]{1,0:T(8,128)(2,1)S(1)} %get-tuple-element.32), channel_id=1, source_target_pairs={{0,16},{8,24},{16,0},{24,8},{1,17},{9,25},{17,1},{25,9},{2,18},{10... | collective-permute-start | bytes 202760 | tf_op jit(solution)/shard_map/ppermute | solution.py:833
  45.5 4.1 %collective-permute-start.2 = (bf16[264,128]{1,0:T(8,128)(2,1)S(1)}, bf16[264,128]{1,0:T(8,128)(2,1)S(1)}, u32[]{:S(2)}, u32[]{:S(2)}) collective-permute-start(bf16[264,128]{1,0:T(8,128)(2,1)S(1)} %get-tuple-element.33), channel_id=1, source_target_pairs={{0,24},{8,16},{16,8},{24,0},{1,25},{9,17},{17,9},{25,1},{2,26},{10... | collective-permute-start | bytes 202760 | tf_op jit(solution)/shard_map/ppermute | solution.py:833
where the time goes:
time: 51.7 us; the launch traced here: 51.4 us
  Pallas kernels  21.5 us (42%)
  blocking collectives  13.1 us (25%)
  starting transfers between devices  9.23 us (18%)
  waiting for transfers between devices  6.49 us (13%)
  between operations  0.97 us (2%)
    all_to_all x1, blocking collectives, kernel_body(): grad = lax.all_to_all(grad, 'ctx', 0, 0, tiled=True)  13.1 us
    all_to_all x1, starting transfers between devices, kernel_body(): msg = lax.all_to_all(msg, 'ctx', 0, 0, tiled=True)  7.29 us
    pallas_call x1, Pallas kernels, kernel_body(): call(functools.partial(gradient_kernel, points, width), [vmem_spec()] * 1...  6.65 us
    pallas_call x1, Pallas kernels, kernel_body(): call(prepare_kernel, [hbm_spec()] * 4 + [any_spec()], [(any_spec(), shape...  5.96 us
    pallas_call x1, Pallas kernels, kernel_body(): call(functools.partial(feature_kernel, points), [vmem_spec()] * 7 + [hbm_...  4.13 us
    all_to_all x1, waiting for transfers between devices, kernel_body(): msg = lax.all_to_all(msg, 'ctx', 0, 0, tiled=True)  3.27 us
    ppermute x3, waiting for transfers between devices, kernel_body(): lax.ppermute(part, 'path', [(p, p ^ step) for p in range(n_path)])  3.23 us
    pallas_call x1, Pallas kernels, kernel_body(): call(pack_kernel, [hbm_spec()] * 4, [(vmem_spec(), shape((n_ctx, tok_rows...  1.96 us
  transfers between devices with their start and end apart: 4, of which 3 were waited for; matrix products, arithmetic and copies ran while one was open for 0% of the time, Pallas kernels for 13%

commit v1 on v0

--- a/solution.py
+++ b/solution.py
@@ -543,6 +543,7 @@
         signal = slice(kind * cols, (kind + 1) * cols)
         found.append([dot(back_ref[side], prod_ref[side, :, signal]) for side in range(RADIX)])
 
+    alphas = [(point + 0.5) / points for point in range(points)]
     carried = [[jnp.zeros((GROUP, share), F32)] * points for _ in range(3)]
     lane, row = iota((GROUP, LANES), 1), iota((GROUP, LANES), 0)
     for start in reversed(range(0, quarter, CHUNK)):
@@ -557,7 +558,10 @@
                 rows = slice(side * quarter + start + offset, side * quarter + start + offset + GROUP)
                 sent = pl.ds(side * block_part + inside, CHUNK)
                 upstream = msg_ref[block, sent, :].astype(F32)[offset : offset + GROUP]
-                sides.append([rows, upstream] + [jnp.zeros((GROUP, share), F32)] * 4)
+                both = pl.ds(side * quarter + start, CHUNK)
+                base = pair_ref[1, both, :].astype(F32)[offset : offset + GROUP]
+                diff = pair_ref[0, both, :].astype(F32)[offset : offset + GROUP] - base
+                sides.append([rows, upstream, base, diff] + [jnp.zeros((GROUP, share), F32)] * 3)
             for point in reversed(range(points)):
                 lanes = slice(point * share, (point + 1) * share)
                 by_tap = []
@@ -577,24 +581,16 @@
                     ahead.append(window[1 : 1 + GROUP])
                 by_tap += [[None, ahead[0], ahead[1]], [None, None, ahead[2]]]
                 for side in range(RADIX):
-                    rows, _, total, sum0, sum1, sum2 = sides[side]
+                    rows, _, base, diff, total, sum_tok, sum_both = sides[side]
                     inv = inv_ref[rows, lanes]
                     along = inv * (by_tap[side][0] + by_tap[side + 1][1] + by_tap[side + 2][2])
                     total = total + along
-                    sum0 = sum0 + along * (inv * inv)
-                    sum1 = sum1 + sum0
-                    sides[side][2:] = [total, sum0, sum1, sum2 + sum1]
+                    along = along * (base + alphas[point] * diff) * (inv * inv)
+                    sides[side][4:] = [total, sum_tok + alphas[point] * along, sum_both + along]
             for side in range(RADIX):
-                _, _, total, sum0, sum1, sum2 = sides[side]
-                rows = pl.ds(side * quarter + start, CHUNK)
-                base = pair_ref[1, rows, :].astype(F32)[offset : offset + GROUP]
-                diff = pair_ref[0, rows, :].astype(F32)[offset : offset + GROUP] - base
-                once = (sum1 - 0.5 * sum0) * (1.0 / points)
-                twice = (2.0 * (sum2 - sum1) + 0.25 * sum0) * (1.0 / points**2)
-                to_tok = base * once + diff * twice
-                to_base = base * sum0 + diff * once - to_tok
+                _, _, _, _, total, sum_tok, sum_both = sides[side]
                 kept[side][offset] = gain * total
-                for kind, value in enumerate((gain * to_tok, gain * to_base)):
+                for kind, value in enumerate((gain * sum_tok, gain * (sum_both - sum_tok))):
                     value = jnp.sum(value, 1, keepdims=True)
                     at = lane == row + (side * block_part + inside + offset)
                     means[kind] = means[kind] + jnp.where(at, value, 0.0)

time: 51.7 us -> 51.7 us (level)
  no operation moved by 1% of the time
where the time goes in v1:
time: 51.7 us; the launch traced here: 51.4 us
  Pallas kernels  21.5 us (42%)
  blocking collectives  13.1 us (25%)
  starting transfers between devices  9.23 us (18%)
  waiting for transfers between devices  6.5 us (13%)
  between operations  0.97 us (2%)
    all_to_all x1, blocking collectives, kernel_body(): grad = lax.all_to_all(grad, 'ctx', 0, 0, tiled=True)  13.1 us
    all_to_all x1, starting transfers between devices, kernel_body(): msg = lax.all_to_all(msg, 'ctx', 0, 0, tiled=True)  7.29 us
    pallas_call x1, Pallas kernels, kernel_body(): call(functools.partial(gradient_kernel, points, width), [vmem_spec()] * 1...  6.61 us
    pallas_call x1, Pallas kernels, kernel_body(): call(prepare_kernel, [hbm_spec()] * 4 + [any_spec()], [(any_spec(), shape...  5.96 us
    pallas_call x1, Pallas kernels, kernel_body(): call(functools.partial(feature_kernel, points), [vmem_spec()] * 7 + [hbm_...  4.13 us
    all_to_all x1, waiting for transfers between devices, kernel_body(): msg = lax.all_to_all(msg, 'ctx', 0, 0, tiled=True)  3.27 us
    ppermute x3, waiting for transfers between devices, kernel_body(): lax.ppermute(part, 'path', [(p, p ^ step) for p in range(n_path)])  3.24 us
    pallas_call x1, Pallas kernels, kernel_body(): call(pack_kernel, [hbm_spec()] * 4, [(vmem_spec(), shape((n_ctx, tok_rows...  1.96 us
  transfers between devices with their start and end apart: 4, of which 3 were waited for; matrix products, arithmetic and copies ran while one was open for 0% of the time, Pallas kernels for 13%

profile of v1, /device:TPU:0, one launch (start us, length us, event | category | flops | bytes accessed | tf_op | source)
XLA Modules:
  0.0 51.4 jit_solution(6155428644376489840)
XLA Ops:
  0.6 2.0 %shard_map.122 = (bf16[8,136,128]{2,1,0:T(8,128)(2,1)}, f32[8,128]{1,0:T(8,128)}) custom-call(s32[1,128]{1,0:T(1,128)} %bitcast.7, s32[1,16]{1,0:T(1,128)} %bitcast.8, s32[1,16]{1,0:T(1,128)} %bitcast.9, bf16[128,4096]{1,0:T(8,128)(2,1)} %cot_hbm.1), custom_call_target="tpu_custom_call" | custom-call | flops 131072 | bytes 1048576 | tf_op jit(solution)/shard_map/pallas_call | solution.py:713
  2.6 7.3 %all-to-all-start = ((bf16[8,136,128]{2,1,0:T(8,128)(2,1)}), bf16[8,136,128]{2,1,0:T(8,128)(2,1)S(1)}, u32[]{:S(2)}, u32[]{:S(2)}) async-start(bf16[8,136,128]{2,1,0:T(8,128)(2,1)} %get-tuple-element.19), calls=%async_computation | async-start | bytes 557056 | tf_op jit(solution)/shard_map/all_to_all | solution.py:736
  9.9 6.0 %shard_map.124 = (f32[8,256,128]{2,1,0:T(8,128)}, bf16[1792,512]{1,0:T(8,128)(2,1)}) custom-call(f32[1024,512]{1,0:T(8,128)} %filt_hbm.1, bf16[4,512,256]{2,1,0:T(8,128)(2,1)} %constant.4.clone.table_hbm.table_ref, bf16[512,4096]{1,0:T(8,128)(2,1)} %embed_ref.1, f32[1,512]{1,0:T(1,128)} %bitcast.10, f32[8,128]{1,0:T(8,128)} %get-tuple-element.18.after_ref.ids_ref), custom_call_target="tpu_custom_call" | custom-call | flops 2147483648 | bytes 4194304 | tf_op jit(solution)/shard_map/pallas_call | solution.py:740
  15.9 0.0 copy-start.1
  15.9 0.0 copy-start.5
  15.9 0.0 copy-start.6
  15.9 3.3 %all-to-all-done.msg_ref = bf16[8,136,128]{2,1,0:T(8,128)(2,1)S(1)} async-done(((bf16[8,136,128]{2,1,0:T(8,128)(2,1)}), bf16[8,136,128]{2,1,0:T(8,128)(2,1)S(1)}, u32[]{:S(2)}, u32[]{:S(2)}) %all-to-all-start) | async-done | bytes 278560 | tf_op jit(solution)/shard_map/all_to_all | solution.py:736
  19.2 0.7 %shard_map.123 = (bf16[1024,512]{1,0:T(8,128)(2,1)S(1)}, bf16[256,512]{1,0:T(8,128)(2,1)S(1)}, bf16[1024,256]{1,0:T(8,128)(2,1)S(1)}) custom-call(bf16[8,136,128]{2,1,0:T(8,128)(2,1)S(1)} %all-to-all-done.msg_ref), custom_call_target="tpu_custom_call" | custom-call | flops 2000000000 | bytes 4000000 | tf_op jit(solution)/shard_map/pallas_call | solution.py:763
  19.9 0.0 copy-done.1
  19.9 0.0 copy-done.5
  19.9 0.0 copy-done.6
  19.9 0.0 copy-start.2
  19.9 0.0 copy-start.3
  19.9 0.0 copy-start.4
  19.9 4.1 %shard_map.125 = (bf16[1024,1024]{1,0:T(8,128)(2,1)S(1)}, f32[1024,512]{1,0:T(8,128)S(1)}, f32[1024,512]{1,0:T(8,128)S(1)}, f32[1024,512]{1,0:T(8,128)S(1)}, bf16[2,1024,128]{2,1,0:T(8,128)(2,1)S(1)}) custom-call(bf16[8,136,128]{2,1,0:T(8,128)(2,1)S(1)} %all-to-all-done.msg_ref, bf16[1024,512]{1,0:T(8,128)(2,1)S(1)} %get-tuple-element.20.hot_ref, ...), custom_call_target="tpu_custom_call" | custom-call | flops 402653184 | bytes 12582912 | tf_op jit(solution)/shard_map/pallas_call | solution.py:777
  24.1 0.0 copy-done.2
  24.1 0.0 copy-done.3
  24.1 0.0 copy-done.4
  24.1 0.0 copy-start
  24.1 0.0 copy-start.7
  24.1 6.6 %shard_map.126.grad_ref = bf16[8,136,128]{2,1,0:T(8,128)(2,1)S(1)} custom-call(bf16[8,136,128]{2,1,0:T(8,128)(2,1)S(1)} %all-to-all-done.msg_ref, bf16[2,1024,128]{2,1,0:T(8,128)(2,1)S(1)} %get-tuple-element.24.pair_ref, bf16[3,3,4096]{2,1,0:T(4,128)(2,1)S(1)} %copy-done.5, f32[1,4096]{1,0:T(1,128)S(1)} %bitcast.6, ...), custom_call_target="tpu_custom_call" | custom-call | flops 2147483648 | bytes 12582912 | tf_op jit(solution)/shard_map/pallas_call | solution.py:796
  30.7 13.1 %all_to_all.10.grad_ref = bf16[8,136,128]{2,1,0:T(8,128)(2,1)S(1)} all-to-all(bf16[8,136,128]{2,1,0:T(8,128)(2,1)S(1)} %shard_map.126.grad_ref), channel_id=1, replica_groups=mesh['path'=4,'ctx'=8] {'ctx'}, dimensions={0} | all-to-all | bytes 557056 | tf_op jit(solution)/shard_map/all_to_all | solution.py:817
  43.9 0.1 collective-permute-start
  44.0 1.5 %collective-permute-start.1 = (bf16[264,128]{1,0:T(8,128)(2,1)S(1)}, bf16[264,128]{1,0:T(8,128)(2,1)S(1)}, u32[]{:S(2)}, u32[]{:S(2)}) collective-permute-start(bf16[264,128]{1,0:T(8,128)(2,1)S(1)} %get-tuple-element.32), channel_id=1, source_target_pairs={{0,16},{8,24},{16,0},{24,8},{1,17},{9,25},{17,1},{25,9},{2,18},{10... | collective-permute-start | bytes 202760 | tf_op jit(solution)/shard_map/ppermute | solution.py:829
  45.5 0.3 collective-permute-start.2
  45.8 0.0 copy-done
  45.8 0.0 copy-done.7
  45.8 0.6 %shard_map.127.own_ref = bf16[2,128,1024]{2,1,0:T(8,128)(2,1)S(1)} custom-call(f32[8,128]{1,0:T(8,128)S(1)} %copy-done.7, bf16[512,4096]{1,0:T(8,128)(2,1)S(1)} %copy-done, bf16[8,136,128]{2,1,0:T(8,128)(2,1)S(1)} %shard_map.126.grad_ref), custom_call_target="tpu_custom_call" | custom-call | flops 268435456 | bytes 1048576 | tf_op jit(solution)/shard_map/pallas_call | solution.py:808
  46.4 0.0 collective-permute-done.refs_1_
  46.4 2.1 %collective-permute-done.1.refs_2_ = bf16[264,128]{1,0:T(8,128)(2,1)S(1)} collective-permute-done((bf16[264,128]{1,0:T(8,128)(2,1)S(1)}, bf16[264,128]{1,0:T(8,128)(2,1)S(1)}, u32[]{:S(2)}, u32[]{:S(2)}) %collective-permute-start.1) | collective-permute-done | bytes 67616 | tf_op jit(solution)/shard_map/ppermute | solution.py:829
  48.5 1.1 %collective-permute-done.2.refs_3_ = bf16[264,128]{1,0:T(8,128)(2,1)S(1)} collective-permute-done((bf16[264,128]{1,0:T(8,128)(2,1)S(1)}, bf16[264,128]{1,0:T(8,128)(2,1)S(1)}, u32[]{:S(2)}, u32[]{:S(2)}) %collective-permute-start.2) | collective-permute-done | bytes 67616 | tf_op jit(solution)/shard_map/ppermute | solution.py:829
  49.6 1.6 %shard_map.129 = (f32[128,1024]{1,0:T(8,128)}, f32[128,1024]{1,0:T(8,128)}) custom-call(bf16[2,128,1024]{2,1,0:T(8,128)(2,1)S(1)} %shard_map.127.own_ref, bf16[264,128]{1,0:T(8,128)(2,1)S(1)} %get-tuple-element.30.refs_0_, bf16[264,128]{1,0:T(8,128)(2,1)S(1)} %collective-permute-done.refs_1_, bf16[264,128]{1,0:T(8,128)(2,1)S(1)} %collective-permute-done.1.refs_2_, ...), custom_call_target="tpu_custom_call" | custom-call | flops 1048576 | bytes 1835008 | tf_op jit(solution)/shard_map/pallas_call | solution.py:834
  (1 shorter events, 0.0 us)
Async XLA Ops:
  2.6 16.6 %all-to-all-start = ((bf16[8,136,128]{2,1,0:T(8,128)(2,1)}), bf16[8,136,128]{2,1,0:T(8,128)(2,1)S(1)}, u32[]{:S(2)}, u32[]{:S(2)}) async-start(bf16[8,136,128]{2,1,0:T(8,128)(2,1)} %get-tuple-element.19), calls=%async_computation | async-start | bytes 557056 | tf_op jit(solution)/shard_map/all_to_all | solution.py:736
  15.9 4.0 %copy-start.1 = (bf16[1792,512]{1,0:T(8,128)(2,1)S(1)}, bf16[1792,512]{1,0:T(8,128)(2,1)}, u32[]{:S(2)}) copy-start(bf16[1792,512]{1,0:T(8,128)(2,1)} %get-tuple-element.23.gram_ref) | copy-start | bytes 5505028
  15.9 4.0 %copy-start.5 = (bf16[3,3,4096]{2,1,0:T(4,128)(2,1)S(1)}, bf16[3,3,4096]{2,1,0:T(4,128)(2,1)}, u32[]{:S(2)}) copy-start(bf16[3,3,4096]{2,1,0:T(4,128)(2,1)} %taps_ref.3) | copy-start | bytes 221188
  15.9 4.0 %copy-start.6 = (f32[4096]{0:T(1024)S(1)}, f32[4096]{0:T(1024)}, u32[]{:S(2)}) copy-start(f32[4096]{0:T(1024)} %param.15) | copy-start | bytes 49156
  19.9 4.2 %copy-start.2 = (bf16[4,512,256]{2,1,0:T(8,128)(2,1)S(1)}, bf16[4,512,256]{2,1,0:T(8,128)(2,1)}, u32[]{:S(2)}) copy-start(bf16[4,512,256]{2,1,0:T(8,128)(2,1)} %constant.4.clone.table_hbm.table_ref) | copy-start | bytes 3145732
  19.9 4.2 %copy-start.3 = (bf16[4,256,512]{2,1,0:T(8,128)(2,1)S(1)}, bf16[4,256,512]{2,1,0:T(8,128)(2,1)}, u32[]{:S(2)}) copy-start(bf16[4,256,512]{2,1,0:T(8,128)(2,1)} %constant.5.clone.back_ref) | copy-start | bytes 3145732
  19.9 4.2 %copy-start.4 = (f32[8,256,128]{2,1,0:T(8,128)S(1)}, f32[8,256,128]{2,1,0:T(8,128)}, u32[]{:S(2)}) copy-start(f32[8,256,128]{2,1,0:T(8,128)} %get-tuple-element.29.spec_ref) | copy-start | bytes 3145732
  24.1 21.7 %copy-start = (bf16[512,4096]{1,0:T(8,128)(2,1)S(1)}, bf16[512,4096]{1,0:T(8,128)(2,1)}, u32[]{:S(2)}) copy-start(bf16[512,4096]{1,0:T(8,128)(2,1)} %embed_ref.1) | copy-start | bytes 12582916
  24.1 21.7 %copy-start.7 = (f32[8,128]{1,0:T(8,128)S(1)}, f32[8,128]{1,0:T(8,128)}, u32[]{:S(2)}) copy-start(f32[8,128]{1,0:T(8,128)} %get-tuple-element.18.after_ref.ids_ref) | copy-start | bytes 12292
  43.9 2.5 %collective-permute-start = (bf16[264,128]{1,0:T(8,128)(2,1)S(1)}, bf16[264,128]{1,0:T(8,128)(2,1)S(1)}, u32[]{:S(2)}, u32[]{:S(2)}) collective-permute-start(bf16[264,128]{1,0:T(8,128)(2,1)S(1)} %get-tuple-element.31), channel_id=1, source_target_pairs={{0,8},{8,0},{16,24},{24,16},{1,9},{9,1},{17,25},{25,17},{2,10},{10... | collective-permute-start | bytes 202760 | tf_op jit(solution)/shard_map/ppermute | solution.py:829
  44.0 4.6 %collective-permute-start.1 = (bf16[264,128]{1,0:T(8,128)(2,1)S(1)}, bf16[264,128]{1,0:T(8,128)(2,1)S(1)}, u32[]{:S(2)}, u32[]{:S(2)}) collective-permute-start(bf16[264,128]{1,0:T(8,128)(2,1)S(1)} %get-tuple-element.32), channel_id=1, source_target_pairs={{0,16},{8,24},{16,0},{24,8},{1,17},{9,25},{17,1},{25,9},{2,18},{10... | collective-permute-start | bytes 202760 | tf_op jit(solution)/shard_map/ppermute | solution.py:829
  45.5 4.1 %collective-permute-start.2 = (bf16[264,128]{1,0:T(8,128)(2,1)S(1)}, bf16[264,128]{1,0:T(8,128)(2,1)S(1)}, u32[]{:S(2)}, u32[]{:S(2)}) collective-permute-start(bf16[264,128]{1,0:T(8,128)(2,1)S(1)} %get-tuple-element.33), channel_id=1, source_target_pairs={{0,24},{8,16},{16,8},{24,0},{1,25},{9,17},{17,9},{25,1},{2,26},{10... | collective-permute-start | bytes 202760 | tf_op jit(solution)/shard_map/ppermute | solution.py:829

commit v2 on v1

--- a/solution.py
+++ b/solution.py
@@ -336,7 +336,7 @@
         after = slice(quarter + start, quarter + start + CHUNK)
         filt = [(spec_ref[2 * part, here, :], spec_ref[2 * part + 1, here, :]) for part in range(RADIX)]
         for point in range(points):
-            lanes = slice(point * share, (point + 1) * share)
+            lanes = slice((kind * points + point) * share, (kind * points + point + 1) * share)
             values = butterfly([(value[here, lanes], value[after, lanes]) for value in found], -1)
             prods = []
             for (real, imag), (filt_real, filt_imag) in zip(values, filt):
@@ -344,7 +344,6 @@
                     prods.append((real * filt_real + imag * filt_imag, imag * filt_real - real * filt_imag))
                 else:
                     prods.append((real * filt_real - imag * filt_imag, imag * filt_real + real * filt_imag))
-            lanes = slice((kind * points + point) * share, (kind * points + point + 1) * share)
             for part, (real, imag) in enumerate(butterfly(prods, 1)):
                 prod_ref[part, here, lanes] = real.astype(BF16)
                 prod_ref[part, after, lanes] = imag.astype(BF16)
@@ -531,17 +530,12 @@
     taps = [taps_ref[f, :, pl.ds(first, share)].astype(F32) for f in range(3)]
     taps = [[taps[f][tap : tap + 1] for tap in range(3)] for f in range(3)]
 
-    found = []
+    spectra = [
+        dot(table_ref[side], signal_ref[side * quarter : (side + 1) * quarter, :]) for side in range(RADIX)
+    ]
     for kind in range(2):
-        signal = slice(kind * cols, (kind + 1) * cols)
-        spectra = [
-            dot(table_ref[side], signal_ref[side * quarter : (side + 1) * quarter, signal])
-            for side in range(RADIX)
-        ]
         multiply_rows(spectra, spec_ref, prod_ref, points, kind)
-    for kind in range(2):
-        signal = slice(kind * cols, (kind + 1) * cols)
-        found.append([dot(back_ref[side], prod_ref[side, :, signal]) for side in range(RADIX)])
+    found = [dot(back_ref[side], prod_ref[side]) for side in range(RADIX)]
 
     alphas = [(point + 0.5) / points for point in range(points)]
     carried = [[jnp.zeros((GROUP, share), F32)] * points for _ in range(3)]
@@ -567,9 +561,9 @@
                 by_tap = []
                 for side in range(RADIX):
                     rows, upstream = sides[side][:2]
-                    grad_z = found[1][side][here, lanes]
+                    grad_z = found[side][here, cols + point * share : cols + (point + 1) * share]
                     grads = (
-                        upstream * found[0][side][here, lanes],
+                        upstream * found[side][here, lanes],
                         grad_z * v_ref[rows, lanes],
                         grad_z * k_ref[rows, lanes],
                     )

time: 51.7 us -> 51.6 us (level)
  no operation moved by 1% of the time
where the time goes in v2:
time: 51.6 us; the launch traced here: 51.3 us
  Pallas kernels  21.5 us (42%)
  blocking collectives  13.1 us (25%)
  starting transfers between devices  9.23 us (18%)
  waiting for transfers between devices  6.49 us (13%)
  between operations  0.97 us (2%)
    all_to_all x1, blocking collectives, kernel_body(): grad = lax.all_to_all(grad, 'ctx', 0, 0, tiled=True)  13.1 us
    all_to_all x1, starting transfers between devices, kernel_body(): msg = lax.all_to_all(msg, 'ctx', 0, 0, tiled=True)  7.29 us
    pallas_call x1, Pallas kernels, kernel_body(): call(functools.partial(gradient_kernel, points, width), [vmem_spec()] * 1...  6.56 us
    pallas_call x1, Pallas kernels, kernel_body(): call(prepare_kernel, [hbm_spec()] * 4 + [any_spec()], [(any_spec(), shape...  5.96 us
    pallas_call x1, Pallas kernels, kernel_body(): call(functools.partial(feature_kernel, points), [vmem_spec()] * 7 + [hbm_...  4.13 us
    all_to_all x1, waiting for transfers between devices, kernel_body(): msg = lax.all_to_all(msg, 'ctx', 0, 0, tiled=True)  3.27 us
    ppermute x3, waiting for transfers between devices, kernel_body(): lax.ppermute(part, 'path', [(p, p ^ step) for p in range(n_path)])  3.23 us
    pallas_call x1, Pallas kernels, kernel_body(): call(pack_kernel, [hbm_spec()] * 4, [(vmem_spec(), shape((n_ctx, tok_rows...  1.96 us
  transfers between devices with their start and end apart: 4, of which 3 were waited for; matrix products, arithmetic and copies ran while one was open for 0% of the time, Pallas kernels for 13%

profile of v2, /device:TPU:0, one launch (start us, length us, event | category | flops | bytes accessed | tf_op | source)
XLA Modules:
  0.0 51.3 jit_solution(969230863160703815)
XLA Ops:
  0.6 2.0 %shard_map.122 = (bf16[8,136,128]{2,1,0:T(8,128)(2,1)}, f32[8,128]{1,0:T(8,128)}) custom-call(s32[1,128]{1,0:T(1,128)} %bitcast.7, s32[1,16]{1,0:T(1,128)} %bitcast.8, s32[1,16]{1,0:T(1,128)} %bitcast.9, bf16[128,4096]{1,0:T(8,128)(2,1)} %cot_hbm.1), custom_call_target="tpu_custom_call" | custom-call | flops 131072 | bytes 1048576 | tf_op jit(solution)/shard_map/pallas_call | solution.py:707
  2.6 7.3 %all-to-all-start = ((bf16[8,136,128]{2,1,0:T(8,128)(2,1)}), bf16[8,136,128]{2,1,0:T(8,128)(2,1)S(1)}, u32[]{:S(2)}, u32[]{:S(2)}) async-start(bf16[8,136,128]{2,1,0:T(8,128)(2,1)} %get-tuple-element.19), calls=%async_computation | async-start | bytes 557056 | tf_op jit(solution)/shard_map/all_to_all | solution.py:730
  9.9 6.0 %shard_map.124 = (f32[8,256,128]{2,1,0:T(8,128)}, bf16[1792,512]{1,0:T(8,128)(2,1)}) custom-call(f32[1024,512]{1,0:T(8,128)} %filt_hbm.1, bf16[4,512,256]{2,1,0:T(8,128)(2,1)} %constant.4.clone.table_hbm.table_ref, bf16[512,4096]{1,0:T(8,128)(2,1)} %embed_ref.1, f32[1,512]{1,0:T(1,128)} %bitcast.10, f32[8,128]{1,0:T(8,128)} %get-tuple-element.18.after_ref.ids_ref), custom_call_target="tpu_custom_call" | custom-call | flops 2147483648 | bytes 4194304 | tf_op jit(solution)/shard_map/pallas_call | solution.py:734
  15.9 0.0 copy-start.1
  15.9 0.0 copy-start.5
  15.9 0.0 copy-start.6
  15.9 3.3 %all-to-all-done.msg_ref = bf16[8,136,128]{2,1,0:T(8,128)(2,1)S(1)} async-done(((bf16[8,136,128]{2,1,0:T(8,128)(2,1)}), bf16[8,136,128]{2,1,0:T(8,128)(2,1)S(1)}, u32[]{:S(2)}, u32[]{:S(2)}) %all-to-all-start) | async-done | bytes 278560 | tf_op jit(solution)/shard_map/all_to_all | solution.py:730
  19.2 0.7 %shard_map.123 = (bf16[1024,512]{1,0:T(8,128)(2,1)S(1)}, bf16[256,512]{1,0:T(8,128)(2,1)S(1)}, bf16[1024,256]{1,0:T(8,128)(2,1)S(1)}) custom-call(bf16[8,136,128]{2,1,0:T(8,128)(2,1)S(1)} %all-to-all-done.msg_ref), custom_call_target="tpu_custom_call" | custom-call | flops 2000000000 | bytes 4000000 | tf_op jit(solution)/shard_map/pallas_call | solution.py:757
  19.9 0.0 copy-done.1
  19.9 0.0 copy-done.5
  19.9 0.0 copy-done.6
  19.9 0.0 copy-start.2
  19.9 0.0 copy-start.3
  19.9 0.0 copy-start.4
  19.9 4.1 %shard_map.125 = (bf16[1024,1024]{1,0:T(8,128)(2,1)S(1)}, f32[1024,512]{1,0:T(8,128)S(1)}, f32[1024,512]{1,0:T(8,128)S(1)}, f32[1024,512]{1,0:T(8,128)S(1)}, bf16[2,1024,128]{2,1,0:T(8,128)(2,1)S(1)}) custom-call(bf16[8,136,128]{2,1,0:T(8,128)(2,1)S(1)} %all-to-all-done.msg_ref, bf16[1024,512]{1,0:T(8,128)(2,1)S(1)} %get-tuple-element.20.hot_ref, ...), custom_call_target="tpu_custom_call" | custom-call | flops 402653184 | bytes 12582912 | tf_op jit(solution)/shard_map/pallas_call | solution.py:771
  24.1 0.0 copy-done.2
  24.1 0.0 copy-done.3
  24.1 0.0 copy-done.4
  24.1 0.0 copy-start
  24.1 0.0 copy-start.7
  24.1 6.6 %shard_map.126.grad_ref = bf16[8,136,128]{2,1,0:T(8,128)(2,1)S(1)} custom-call(bf16[8,136,128]{2,1,0:T(8,128)(2,1)S(1)} %all-to-all-done.msg_ref, bf16[2,1024,128]{2,1,0:T(8,128)(2,1)S(1)} %get-tuple-element.24.pair_ref, bf16[3,3,4096]{2,1,0:T(4,128)(2,1)S(1)} %copy-done.5, f32[1,4096]{1,0:T(1,128)S(1)} %bitcast.6, ...), custom_call_target="tpu_custom_call" | custom-call | flops 2147483648 | bytes 12582912 | tf_op jit(solution)/shard_map/pallas_call | solution.py:790
  30.7 13.1 %all_to_all.10.grad_ref = bf16[8,136,128]{2,1,0:T(8,128)(2,1)S(1)} all-to-all(bf16[8,136,128]{2,1,0:T(8,128)(2,1)S(1)} %shard_map.126.grad_ref), channel_id=1, replica_groups=mesh['path'=4,'ctx'=8] {'ctx'}, dimensions={0} | all-to-all | bytes 557056 | tf_op jit(solution)/shard_map/all_to_all | solution.py:811
  43.8 0.1 collective-permute-start
  43.9 1.6 %collective-permute-start.1 = (bf16[264,128]{1,0:T(8,128)(2,1)S(1)}, bf16[264,128]{1,0:T(8,128)(2,1)S(1)}, u32[]{:S(2)}, u32[]{:S(2)}) collective-permute-start(bf16[264,128]{1,0:T(8,128)(2,1)S(1)} %get-tuple-element.32), channel_id=1, source_target_pairs={{0,16},{8,24},{16,0},{24,8},{1,17},{9,25},{17,1},{25,9},{2,18},{10... | collective-permute-start | bytes 202760 | tf_op jit(solution)/shard_map/ppermute | solution.py:823
  45.4 0.3 collective-permute-start.2
  45.7 0.0 copy-done
  45.7 0.0 copy-done.7
  45.7 0.6 %shard_map.127.own_ref = bf16[2,128,1024]{2,1,0:T(8,128)(2,1)S(1)} custom-call(f32[8,128]{1,0:T(8,128)S(1)} %copy-done.7, bf16[512,4096]{1,0:T(8,128)(2,1)S(1)} %copy-done, bf16[8,136,128]{2,1,0:T(8,128)(2,1)S(1)} %shard_map.126.grad_ref), custom_call_target="tpu_custom_call" | custom-call | flops 268435456 | bytes 1048576 | tf_op jit(solution)/shard_map/pallas_call | solution.py:802
  46.3 0.0 collective-permute-done.refs_1_
  46.3 2.1 %collective-permute-done.1.refs_2_ = bf16[264,128]{1,0:T(8,128)(2,1)S(1)} collective-permute-done((bf16[264,128]{1,0:T(8,128)(2,1)S(1)}, bf16[264,128]{1,0:T(8,128)(2,1)S(1)}, u32[]{:S(2)}, u32[]{:S(2)}) %collective-permute-start.1) | collective-permute-done | bytes 67616 | tf_op jit(solution)/shard_map/ppermute | solution.py:823
  48.5 1.1 %collective-permute-done.2.refs_3_ = bf16[264,128]{1,0:T(8,128)(2,1)S(1)} collective-permute-done((bf16[264,128]{1,0:T(8,128)(2,1)S(1)}, bf16[264,128]{1,0:T(8,128)(2,1)S(1)}, u32[]{:S(2)}, u32[]{:S(2)}) %collective-permute-start.2) | collective-permute-done | bytes 67616 | tf_op jit(solution)/shard_map/ppermute | solution.py:823
  49.5 1.6 %shard_map.129 = (f32[128,1024]{1,0:T(8,128)}, f32[128,1024]{1,0:T(8,128)}) custom-call(bf16[2,128,1024]{2,1,0:T(8,128)(2,1)S(1)} %shard_map.127.own_ref, bf16[264,128]{1,0:T(8,128)(2,1)S(1)} %get-tuple-element.30.refs_0_, bf16[264,128]{1,0:T(8,128)(2,1)S(1)} %collective-permute-done.refs_1_, bf16[264,128]{1,0:T(8,128)(2,1)S(1)} %collective-permute-done.1.refs_2_, ...), custom_call_target="tpu_custom_call" | custom-call | flops 1048576 | bytes 1835008 | tf_op jit(solution)/shard_map/pallas_call | solution.py:828
  (1 shorter events, 0.0 us)
Async XLA Ops:
  2.6 16.6 %all-to-all-start = ((bf16[8,136,128]{2,1,0:T(8,128)(2,1)}), bf16[8,136,128]{2,1,0:T(8,128)(2,1)S(1)}, u32[]{:S(2)}, u32[]{:S(2)}) async-start(bf16[8,136,128]{2,1,0:T(8,128)(2,1)} %get-tuple-element.19), calls=%async_computation | async-start | bytes 557056 | tf_op jit(solution)/shard_map/all_to_all | solution.py:730
  15.9 4.0 %copy-start.1 = (bf16[1792,512]{1,0:T(8,128)(2,1)S(1)}, bf16[1792,512]{1,0:T(8,128)(2,1)}, u32[]{:S(2)}) copy-start(bf16[1792,512]{1,0:T(8,128)(2,1)} %get-tuple-element.23.gram_ref) | copy-start | bytes 5505028
  15.9 4.0 %copy-start.5 = (bf16[3,3,4096]{2,1,0:T(4,128)(2,1)S(1)}, bf16[3,3,4096]{2,1,0:T(4,128)(2,1)}, u32[]{:S(2)}) copy-start(bf16[3,3,4096]{2,1,0:T(4,128)(2,1)} %taps_ref.3) | copy-start | bytes 221188
  15.9 4.0 %copy-start.6 = (f32[4096]{0:T(1024)S(1)}, f32[4096]{0:T(1024)}, u32[]{:S(2)}) copy-start(f32[4096]{0:T(1024)} %param.15) | copy-start | bytes 49156
  19.9 4.2 %copy-start.2 = (bf16[4,512,256]{2,1,0:T(8,128)(2,1)S(1)}, bf16[4,512,256]{2,1,0:T(8,128)(2,1)}, u32[]{:S(2)}) copy-start(bf16[4,512,256]{2,1,0:T(8,128)(2,1)} %constant.4.clone.table_hbm.table_ref) | copy-start | bytes 3145732
  19.9 4.2 %copy-start.3 = (bf16[4,256,512]{2,1,0:T(8,128)(2,1)S(1)}, bf16[4,256,512]{2,1,0:T(8,128)(2,1)}, u32[]{:S(2)}) copy-start(bf16[4,256,512]{2,1,0:T(8,128)(2,1)} %constant.5.clone.back_ref) | copy-start | bytes 3145732
  19.9 4.2 %copy-start.4 = (f32[8,256,128]{2,1,0:T(8,128)S(1)}, f32[8,256,128]{2,1,0:T(8,128)}, u32[]{:S(2)}) copy-start(f32[8,256,128]{2,1,0:T(8,128)} %get-tuple-element.29.spec_ref) | copy-start | bytes 3145732
  24.1 21.6 %copy-start = (bf16[512,4096]{1,0:T(8,128)(2,1)S(1)}, bf16[512,4096]{1,0:T(8,128)(2,1)}, u32[]{:S(2)}) copy-start(bf16[512,4096]{1,0:T(8,128)(2,1)} %embed_ref.1) | copy-start | bytes 12582916
  24.1 21.6 %copy-start.7 = (f32[8,128]{1,0:T(8,128)S(1)}, f32[8,128]{1,0:T(8,128)}, u32[]{:S(2)}) copy-start(f32[8,128]{1,0:T(8,128)} %get-tuple-element.18.after_ref.ids_ref) | copy-start | bytes 12292
  43.8 2.5 %collective-permute-start = (bf16[264,128]{1,0:T(8,128)(2,1)S(1)}, bf16[264,128]{1,0:T(8,128)(2,1)S(1)}, u32[]{:S(2)}, u32[]{:S(2)}) collective-permute-start(bf16[264,128]{1,0:T(8,128)(2,1)S(1)} %get-tuple-element.31), channel_id=1, source_target_pairs={{0,8},{8,0},{16,24},{24,16},{1,9},{9,1},{17,25},{25,17},{2,10},{10... | collective-permute-start | bytes 202760 | tf_op jit(solution)/shard_map/ppermute | solution.py:823
  43.9 4.6 %collective-permute-start.1 = (bf16[264,128]{1,0:T(8,128)(2,1)S(1)}, bf16[264,128]{1,0:T(8,128)(2,1)S(1)}, u32[]{:S(2)}, u32[]{:S(2)}) collective-permute-start(bf16[264,128]{1,0:T(8,128)(2,1)S(1)} %get-tuple-element.32), channel_id=1, source_target_pairs={{0,16},{8,24},{16,0},{24,8},{1,17},{9,25},{17,1},{25,9},{2,18},{10... | collective-permute-start | bytes 202760 | tf_op jit(solution)/shard_map/ppermute | solution.py:823
  45.4 4.1 %collective-permute-start.2 = (bf16[264,128]{1,0:T(8,128)(2,1)S(1)}, bf16[264,128]{1,0:T(8,128)(2,1)S(1)}, u32[]{:S(2)}, u32[]{:S(2)}) collective-permute-start(bf16[264,128]{1,0:T(8,128)(2,1)S(1)} %get-tuple-element.33), channel_id=1, source_target_pairs={{0,24},{8,16},{16,8},{24,0},{1,25},{9,17},{17,9},{25,1},{2,26},{10... | collective-permute-start | bytes 202760 | tf_op jit(solution)/shard_map/ppermute | solution.py:823

commit v3 on v2

--- a/solution.py
+++ b/solution.py
@@ -12,7 +12,7 @@
 LANES = 128
 GROUP = 8
 RADIX = 4
-LOOK_ROWS = 256
+LOOK_ROWS = 1024
 CHUNK = 16
 EPS = 1e-06
 CANCEL = 0.004

time: 51.6 us -> 51.6 us (level)
  no operation moved by 1% of the time
where the time goes in v3:
time: 51.6 us; the launch traced here: 51.3 us
  Pallas kernels  21.5 us (42%)
  blocking collectives  13.1 us (25%)
  starting transfers between devices  9.23 us (18%)
  waiting for transfers between devices  6.49 us (13%)
  between operations  0.97 us (2%)
    all_to_all x1, blocking collectives, kernel_body(): grad = lax.all_to_all(grad, 'ctx', 0, 0, tiled=True)  13.1 us
    all_to_all x1, starting transfers between devices, kernel_body(): msg = lax.all_to_all(msg, 'ctx', 0, 0, tiled=True)  7.29 us
    pallas_call x1, Pallas kernels, kernel_body(): call(functools.partial(gradient_kernel, points, width), [vmem_spec()] * 1...  6.55 us
    pallas_call x1, Pallas kernels, kernel_body(): call(prepare_kernel, [hbm_spec()] * 4 + [any_spec()], [(any_spec(), shape...  5.96 us
    pallas_call x1, Pallas kernels, kernel_body(): call(functools.partial(feature_kernel, points), [vmem_spec()] * 7 + [hbm_...  4.17 us
    all_to_all x1, waiting for transfers between devices, kernel_body(): msg = lax.all_to_all(msg, 'ctx', 0, 0, tiled=True)  3.27 us
    ppermute x3, waiting for transfers between devices, kernel_body(): lax.ppermute(part, 'path', [(p, p ^ step) for p in range(n_path)])  3.22 us
    pallas_call x1, Pallas kernels, kernel_body(): call(pack_kernel, [hbm_spec()] * 4, [(vmem_spec(), shape((n_ctx, tok_rows...  1.96 us
  transfers between devices with their start and end apart: 4, of which 3 were waited for; matrix products, arithmetic and copies ran while one was open for 0% of the time, Pallas kernels for 13%

profile of v3, /device:TPU:0, one launch (start us, length us, event | category | flops | bytes accessed | tf_op | source)
XLA Modules:
  0.0 51.3 jit_solution(6858639655605614495)
XLA Ops:
  0.6 2.0 %shard_map.122 = (bf16[8,136,128]{2,1,0:T(8,128)(2,1)}, f32[8,128]{1,0:T(8,128)}) custom-call(s32[1,128]{1,0:T(1,128)} %bitcast.7, s32[1,16]{1,0:T(1,128)} %bitcast.8, s32[1,16]{1,0:T(1,128)} %bitcast.9, bf16[128,4096]{1,0:T(8,128)(2,1)} %cot_hbm.1), custom_call_target="tpu_custom_call" | custom-call | flops 131072 | bytes 1048576 | tf_op jit(solution)/shard_map/pallas_call | solution.py:707
  2.6 7.3 %all-to-all-start = ((bf16[8,136,128]{2,1,0:T(8,128)(2,1)}), bf16[8,136,128]{2,1,0:T(8,128)(2,1)S(1)}, u32[]{:S(2)}, u32[]{:S(2)}) async-start(bf16[8,136,128]{2,1,0:T(8,128)(2,1)} %get-tuple-element.19), calls=%async_computation | async-start | bytes 557056 | tf_op jit(solution)/shard_map/all_to_all | solution.py:730
  9.9 6.0 %shard_map.124 = (f32[8,256,128]{2,1,0:T(8,128)}, bf16[1792,512]{1,0:T(8,128)(2,1)}) custom-call(f32[1024,512]{1,0:T(8,128)} %filt_hbm.1, bf16[4,512,256]{2,1,0:T(8,128)(2,1)} %constant.4.clone.table_hbm.table_ref, bf16[512,4096]{1,0:T(8,128)(2,1)} %embed_ref.1, f32[1,512]{1,0:T(1,128)} %bitcast.10, f32[8,128]{1,0:T(8,128)} %get-tuple-element.18.after_ref.ids_ref), custom_call_target="tpu_custom_call" | custom-call | flops 2147483648 | bytes 4194304 | tf_op jit(solution)/shard_map/pallas_call | solution.py:734
  15.9 0.0 copy-start.1
  15.9 0.0 copy-start.5
  15.9 0.0 copy-start.6
  15.9 3.3 %all-to-all-done.msg_ref = bf16[8,136,128]{2,1,0:T(8,128)(2,1)S(1)} async-done(((bf16[8,136,128]{2,1,0:T(8,128)(2,1)}), bf16[8,136,128]{2,1,0:T(8,128)(2,1)S(1)}, u32[]{:S(2)}, u32[]{:S(2)}) %all-to-all-start) | async-done | bytes 278560 | tf_op jit(solution)/shard_map/all_to_all | solution.py:730
  19.2 0.7 %shard_map.123 = (bf16[1024,512]{1,0:T(8,128)(2,1)S(1)}, bf16[256,512]{1,0:T(8,128)(2,1)S(1)}, bf16[1024,256]{1,0:T(8,128)(2,1)S(1)}) custom-call(bf16[8,136,128]{2,1,0:T(8,128)(2,1)S(1)} %all-to-all-done.msg_ref), custom_call_target="tpu_custom_call" | custom-call | flops 2000000000 | bytes 4000000 | tf_op jit(solution)/shard_map/pallas_call | solution.py:757
  19.9 0.0 copy-done.1
  19.9 0.0 copy-done.5
  19.9 0.0 copy-done.6
  19.9 0.0 copy-start.2
  19.9 0.0 copy-start.3
  19.9 0.0 copy-start.4
  19.9 4.2 %shard_map.125 = (bf16[1024,1024]{1,0:T(8,128)(2,1)S(1)}, f32[1024,512]{1,0:T(8,128)S(1)}, f32[1024,512]{1,0:T(8,128)S(1)}, f32[1024,512]{1,0:T(8,128)S(1)}, bf16[2,1024,128]{2,1,0:T(8,128)(2,1)S(1)}) custom-call(bf16[8,136,128]{2,1,0:T(8,128)(2,1)S(1)} %all-to-all-done.msg_ref, bf16[1024,512]{1,0:T(8,128)(2,1)S(1)} %get-tuple-element.20.hot_ref, ...), custom_call_target="tpu_custom_call" | custom-call | flops 402653184 | bytes 12582912 | tf_op jit(solution)/shard_map/pallas_call | solution.py:771
  24.1 0.0 copy-done.2
  24.1 0.0 copy-done.3
  24.1 0.0 copy-done.4
  24.1 0.0 copy-start
  24.1 0.0 copy-start.7
  24.2 6.6 %shard_map.126.grad_ref = bf16[8,136,128]{2,1,0:T(8,128)(2,1)S(1)} custom-call(bf16[8,136,128]{2,1,0:T(8,128)(2,1)S(1)} %all-to-all-done.msg_ref, bf16[2,1024,128]{2,1,0:T(8,128)(2,1)S(1)} %get-tuple-element.24.pair_ref, bf16[3,3,4096]{2,1,0:T(4,128)(2,1)S(1)} %copy-done.5, f32[1,4096]{1,0:T(1,128)S(1)} %bitcast.6, ...), custom_call_target="tpu_custom_call" | custom-call | flops 2147483648 | bytes 12582912 | tf_op jit(solution)/shard_map/pallas_call | solution.py:790
  30.7 13.1 %all_to_all.10.grad_ref = bf16[8,136,128]{2,1,0:T(8,128)(2,1)S(1)} all-to-all(bf16[8,136,128]{2,1,0:T(8,128)(2,1)S(1)} %shard_map.126.grad_ref), channel_id=1, replica_groups=mesh['path'=4,'ctx'=8] {'ctx'}, dimensions={0} | all-to-all | bytes 557056 | tf_op jit(solution)/shard_map/all_to_all | solution.py:811
  43.8 0.1 collective-permute-start
  43.9 1.6 %collective-permute-start.1 = (bf16[264,128]{1,0:T(8,128)(2,1)S(1)}, bf16[264,128]{1,0:T(8,128)(2,1)S(1)}, u32[]{:S(2)}, u32[]{:S(2)}) collective-permute-start(bf16[264,128]{1,0:T(8,128)(2,1)S(1)} %get-tuple-element.32), channel_id=1, source_target_pairs={{0,16},{8,24},{16,0},{24,8},{1,17},{9,25},{17,1},{25,9},{2,18},{10... | collective-permute-start | bytes 202760 | tf_op jit(solution)/shard_map/ppermute | solution.py:823
  45.5 0.3 collective-permute-start.2
  45.8 0.0 copy-done
  45.8 0.0 copy-done.7
  45.8 0.6 %shard_map.127.own_ref = bf16[2,128,1024]{2,1,0:T(8,128)(2,1)S(1)} custom-call(f32[8,128]{1,0:T(8,128)S(1)} %copy-done.7, bf16[512,4096]{1,0:T(8,128)(2,1)S(1)} %copy-done, bf16[8,136,128]{2,1,0:T(8,128)(2,1)S(1)} %shard_map.126.grad_ref), custom_call_target="tpu_custom_call" | custom-call | flops 268435456 | bytes 1048576 | tf_op jit(solution)/shard_map/pallas_call | solution.py:802
  46.3 0.0 collective-permute-done.refs_1_
  46.3 2.1 %collective-permute-done.1.refs_2_ = bf16[264,128]{1,0:T(8,128)(2,1)S(1)} collective-permute-done((bf16[264,128]{1,0:T(8,128)(2,1)S(1)}, bf16[264,128]{1,0:T(8,128)(2,1)S(1)}, u32[]{:S(2)}, u32[]{:S(2)}) %collective-permute-start.1) | collective-permute-done | bytes 67616 | tf_op jit(solution)/shard_map/ppermute | solution.py:823
  48.5 1.1 %collective-permute-done.2.refs_3_ = bf16[264,128]{1,0:T(8,128)(2,1)S(1)} collective-permute-done((bf16[264,128]{1,0:T(8,128)(2,1)S(1)}, bf16[264,128]{1,0:T(8,128)(2,1)S(1)}, u32[]{:S(2)}, u32[]{:S(2)}) %collective-permute-start.2) | collective-permute-done | bytes 67616 | tf_op jit(solution)/shard_map/ppermute | solution.py:823
  49.6 1.6 %shard_map.129 = (f32[128,1024]{1,0:T(8,128)}, f32[128,1024]{1,0:T(8,128)}) custom-call(bf16[2,128,1024]{2,1,0:T(8,128)(2,1)S(1)} %shard_map.127.own_ref, bf16[264,128]{1,0:T(8,128)(2,1)S(1)} %get-tuple-element.30.refs_0_, bf16[264,128]{1,0:T(8,128)(2,1)S(1)} %collective-permute-done.refs_1_, bf16[264,128]{1,0:T(8,128)(2,1)S(1)} %collective-permute-done.1.refs_2_, ...), custom_call_target="tpu_custom_call" | custom-call | flops 1048576 | bytes 1835008 | tf_op jit(solution)/shard_map/pallas_call | solution.py:828
  (1 shorter events, 0.0 us)
Async XLA Ops:
  2.6 16.6 %all-to-all-start = ((bf16[8,136,128]{2,1,0:T(8,128)(2,1)}), bf16[8,136,128]{2,1,0:T(8,128)(2,1)S(1)}, u32[]{:S(2)}, u32[]{:S(2)}) async-start(bf16[8,136,128]{2,1,0:T(8,128)(2,1)} %get-tuple-element.19), calls=%async_computation | async-start | bytes 557056 | tf_op jit(solution)/shard_map/all_to_all | solution.py:730
  15.9 4.0 %copy-start.1 = (bf16[1792,512]{1,0:T(8,128)(2,1)S(1)}, bf16[1792,512]{1,0:T(8,128)(2,1)}, u32[]{:S(2)}) copy-start(bf16[1792,512]{1,0:T(8,128)(2,1)} %get-tuple-element.23.gram_ref) | copy-start | bytes 5505028
  15.9 4.0 %copy-start.5 = (bf16[3,3,4096]{2,1,0:T(4,128)(2,1)S(1)}, bf16[3,3,4096]{2,1,0:T(4,128)(2,1)}, u32[]{:S(2)}) copy-start(bf16[3,3,4096]{2,1,0:T(4,128)(2,1)} %taps_ref.3) | copy-start | bytes 221188
  15.9 4.0 %copy-start.6 = (f32[4096]{0:T(1024)S(1)}, f32[4096]{0:T(1024)}, u32[]{:S(2)}) copy-start(f32[4096]{0:T(1024)} %param.15) | copy-start | bytes 49156
  19.9 4.2 %copy-start.2 = (bf16[4,512,256]{2,1,0:T(8,128)(2,1)S(1)}, bf16[4,512,256]{2,1,0:T(8,128)(2,1)}, u32[]{:S(2)}) copy-start(bf16[4,512,256]{2,1,0:T(8,128)(2,1)} %constant.4.clone.table_hbm.table_ref) | copy-start | bytes 3145732
  19.9 4.2 %copy-start.3 = (bf16[4,256,512]{2,1,0:T(8,128)(2,1)S(1)}, bf16[4,256,512]{2,1,0:T(8,128)(2,1)}, u32[]{:S(2)}) copy-start(bf16[4,256,512]{2,1,0:T(8,128)(2,1)} %constant.5.clone.back_ref) | copy-start | bytes 3145732
  19.9 4.2 %copy-start.4 = (f32[8,256,128]{2,1,0:T(8,128)S(1)}, f32[8,256,128]{2,1,0:T(8,128)}, u32[]{:S(2)}) copy-start(f32[8,256,128]{2,1,0:T(8,128)} %get-tuple-element.29.spec_ref) | copy-start | bytes 3145732
  24.1 21.6 %copy-start = (bf16[512,4096]{1,0:T(8,128)(2,1)S(1)}, bf16[512,4096]{1,0:T(8,128)(2,1)}, u32[]{:S(2)}) copy-start(bf16[512,4096]{1,0:T(8,128)(2,1)} %embed_ref.1) | copy-start | bytes 12582916
  24.1 21.6 %copy-start.7 = (f32[8,128]{1,0:T(8,128)S(1)}, f32[8,128]{1,0:T(8,128)}, u32[]{:S(2)}) copy-start(f32[8,128]{1,0:T(8,128)} %get-tuple-element.18.after_ref.ids_ref) | copy-start | bytes 12292
  43.8 2.5 %collective-permute-start = (bf16[264,128]{1,0:T(8,128)(2,1)S(1)}, bf16[264,128]{1,0:T(8,128)(2,1)S(1)}, u32[]{:S(2)}, u32[]{:S(2)}) collective-permute-start(bf16[264,128]{1,0:T(8,128)(2,1)S(1)} %get-tuple-element.31), channel_id=1, source_target_pairs={{0,8},{8,0},{16,24},{24,16},{1,9},{9,1},{17,25},{25,17},{2,10},{10... | collective-permute-start | bytes 202760 | tf_op jit(solution)/shard_map/ppermute | solution.py:823
  43.9 4.6 %collective-permute-start.1 = (bf16[264,128]{1,0:T(8,128)(2,1)S(1)}, bf16[264,128]{1,0:T(8,128)(2,1)S(1)}, u32[]{:S(2)}, u32[]{:S(2)}) collective-permute-start(bf16[264,128]{1,0:T(8,128)(2,1)S(1)} %get-tuple-element.32), channel_id=1, source_target_pairs={{0,16},{8,24},{16,0},{24,8},{1,17},{9,25},{17,1},{25,9},{2,18},{10... | collective-permute-start | bytes 202760 | tf_op jit(solution)/shard_map/ppermute | solution.py:823
  45.5 4.1 %collective-permute-start.2 = (bf16[264,128]{1,0:T(8,128)(2,1)S(1)}, bf16[264,128]{1,0:T(8,128)(2,1)S(1)}, u32[]{:S(2)}, u32[]{:S(2)}) collective-permute-start(bf16[264,128]{1,0:T(8,128)(2,1)S(1)} %get-tuple-element.33), channel_id=1, source_target_pairs={{0,24},{8,16},{16,8},{24,0},{1,25},{9,17},{17,9},{25,1},{2,26},{10... | collective-permute-start | bytes 202760 | tf_op jit(solution)/shard_map/ppermute | solution.py:823
